TPU v7x, 32 devices: a whole 2x2x4 slice. The times are simulated.
32 devices in a mesh: rep: 4 (over z), exp: 8 (over y, x, core).
Axes of the slice: x: 2, y: 2, z: 4, core: 2. Of those that a mesh axis runs over, the one named last changes fastest.
Arguments:
- tokens: bfloat16 [16384, 1024], P(('rep', 'exp')), may hold values from -6 to 6
- routes: int32 [16384, 1], P(('rep', 'exp')), may hold values from 0 to 7; in each aligned block of 512 rows (0 to 511, 512 to 1023, ...) at most 64 rows name the same one
- lengths: int32 [8], replicated, may hold values from 1024 to 2048
- centroids: float32 [8, 1024], P('exp'), may hold values from -0.125 to 0.125
- norm_gains: float32 [8, 2, 1024], P('exp'), may hold values from 0.1 to 1.9
- norm_biases: float32 [8, 2, 1024], P('exp'), may hold values from -4 to 4
- w_in: bfloat16 [8, 2, 1024, 4096], P('exp', None, None, 'rep'), may hold values from -0.1875 to 0.1875
- in_biases: float32 [8, 2, 4096], P('exp'), may hold values from -4 to 4
- w_out: bfloat16 [8, 2, 4096, 1024], P('exp', None, 'rep'), may hold values from -0.09375 to 0.09375
- out_biases: float32 [8, 2, 1024], P('exp'), may hold values from -4 to 4
- cotangent: bfloat16 [16384, 1024], P(('rep', 'exp')), may hold values from -6 to 6
Outputs:
- mixed: bfloat16 [16384, 1024], P(('rep', 'exp'))
- tokens_grad: bfloat16 [16384, 1024], P(('rep', 'exp'))
- centroid_grad: float32 [8, 1024], P('exp')
- gain_grad: float32 [8, 2, 1024], P('exp')
- norm_bias_grad: float32 [8, 2, 1024], P('exp')
- w_in_grad: float32 [8, 2, 1024, 4096], P('exp', None, None, 'rep')
- in_bias_grad: float32 [8, 2, 4096], P('exp')
- w_out_grad: float32 [8, 2, 4096, 1024], P('exp', None, 'rep')
- out_bias_grad: float32 [8, 2, 1024], P('exp')
Inputs may be any that keep to these rules, and one draw needn't show every extreme that they name: `routes`: within the token slots of one device, each expert is named by exactly 64 slots.
All inputs are finite; a program needn't handle non-finite values.
Results may differ from a plain program's by a relative error of at most 0.0068.
Values may be sent and summed in bfloat16 or wider, within the bound.
A program may use at most 256 MiB of HBM per device.

v0:
```python
import jax
import jax.numpy as jnp
from jax import lax
from jax.sharding import PartitionSpec as P

SLOT = 2048


eps = 1e-05


def layer_norm(values, gain, bias):
    center = values - jnp.mean(values, -1, keepdims=True)
    spread = jnp.mean(center * center, -1, keepdims=True)
    return center * lax.rsqrt(spread + eps) * gain + bias


def contract_rows(left, right):
    return lax.dot_general(
        left, right, (((0,), (0,)), ((), ())), preferred_element_type=jnp.float32
    )


def contract_cols(left, right):
    return lax.dot_general(
        left, right, (((1,), (1,)), ((), ())), preferred_element_type=jnp.float32
    )


def shards(
    tokens,
    routes,
    lengths,
    centroids,
    norm_gains,
    norm_biases,
    w_in,
    in_biases,
    w_out,
    out_biases,
    cotangent,
):
    n_exp = lax.axis_size("exp")
    tok_rows = tokens.shape[0]
    cap = tok_rows // n_exp
    device = lax.axis_index(("rep", "exp"))
    positions = device * tok_rows + lax.iota(jnp.int32, tok_rows)
    seq_ids = positions // SLOT
    seq_table = lax.iota(jnp.int32, lengths.shape[0])
    seq_len = jnp.sum(jnp.where(seq_ids[:, None] == seq_table[None, :], lengths[None, :], 0), 1)
    live = (positions % SLOT < seq_len).astype(jnp.float32)[:, None]
    route = routes[:, 0]
    hits = (route[:, None] == lax.iota(jnp.int32, n_exp)[None, :]).astype(jnp.int32)
    before = jnp.cumsum(hits, 0) - hits
    target = route * cap + jnp.sum(before * hits, 1)
    outgoing = jnp.zeros_like(tokens).at[target].set(tokens)
    received = lax.all_to_all(outgoing, "exp", split_axis=0, concat_axis=0, tiled=True)
    expert_in = received.astype(jnp.float32)
    w_in_full, w_out_full = (
        lax.all_gather(w_in, "rep", axis=3, tiled=True),
        lax.all_gather(w_out, "rep", axis=2, tiled=True),
    )

    def sub_forward(values, k):
        normed_low = layer_norm(values, norm_gains[0, k], norm_biases[0, k]).astype(jnp.bfloat16)
        inner = (
            jnp.dot(normed_low, w_in_full[0, k], preferred_element_type=jnp.float32)
            + in_biases[0, k]
        )
        act_low = jax.nn.gelu(inner).astype(jnp.bfloat16)
        outer = jnp.dot(act_low, w_out_full[0, k], preferred_element_type=jnp.float32)
        return (values + outer + out_biases[0, k], (values, normed_low, inner, act_low))

    middle, kept_first = sub_forward(expert_in, 0)
    upper, kept_second = sub_forward(middle, 1)
    centroid = centroids[0]
    gate = jax.nn.sigmoid(jnp.sum(expert_in * centroid, -1))[:, None]
    result = (gate * upper).astype(jnp.bfloat16)
    returned = lax.all_to_all(result, "exp", split_axis=0, concat_axis=0, tiled=True)
    mixed = (tokens.astype(jnp.float32) + live * returned[target].astype(jnp.float32)).astype(
        jnp.bfloat16
    )
    grad_out = (live * cotangent.astype(jnp.float32)).astype(jnp.bfloat16)
    grad_send = jnp.zeros_like(cotangent).at[target].set(grad_out)
    grad_recv = lax.all_to_all(grad_send, "exp", split_axis=0, concat_axis=0, tiled=True).astype(
        jnp.float32
    )
    grad_upper = gate * grad_recv
    grad_logit = jnp.sum(grad_recv * upper, -1, keepdims=True) * gate * (1.0 - gate)
    grad_centroid = jnp.sum(grad_logit * expert_in, 0)
    grad_gate_in = grad_logit * centroid
    first_mats, second_mats = (w_in_full, w_out_full)

    def sub_backward(grad_top, kept, k):
        values, normed_low, inner, act_low = kept
        grad_outer = grad_top.astype(jnp.bfloat16)
        grad_second = contract_rows(act_low, grad_outer)
        grad_sbias = jnp.sum(grad_top, 0)
        grad_act = contract_cols(grad_outer, second_mats[0, k])
        gelu_pull = jax.vjp(jax.nn.gelu, inner)[1]
        grad_inner = gelu_pull(grad_act)[0]
        grad_fbias = jnp.sum(grad_inner, 0)
        grad_inner_low = grad_inner.astype(jnp.bfloat16)
        grad_first = contract_rows(normed_low, grad_inner_low)
        grad_normed = contract_cols(grad_inner_low, first_mats[0, k])
        norm_pull = jax.vjp(layer_norm, values, norm_gains[0, k], norm_biases[0, k])[1]
        grad_values, grad_gain, grad_nbias = norm_pull(grad_normed)
        return (
            grad_top + grad_values,
            (grad_first, grad_second),
            (grad_gain, grad_nbias, grad_fbias, grad_sbias),
        )

    grad_middle, large_second, small_second = sub_backward(grad_upper, kept_second, 1)
    grad_input, large_first, small_first = sub_backward(grad_middle, kept_first, 0)
    stacked_in = jnp.stack([large_first[0], large_second[0]], 0)[None]
    stacked_out = jnp.stack([large_first[1], large_second[1]], 0)[None]
    w_in_grad, w_out_grad = (
        lax.psum_scatter(stacked_in, "rep", scatter_dimension=3, tiled=True),
        lax.psum_scatter(stacked_out, "rep", scatter_dimension=2, tiled=True),
    )
    grad_local = (grad_input + grad_gate_in).astype(jnp.bfloat16)
    grad_back = lax.all_to_all(grad_local, "exp", split_axis=0, concat_axis=0, tiled=True)
    tokens_grad = (cotangent.astype(jnp.float32) + grad_back[target].astype(jnp.float32)).astype(
        jnp.bfloat16
    )
    gains_local = jnp.stack([small_first[0], small_second[0]], 0)[None]
    nbias_local = jnp.stack([small_first[1], small_second[1]], 0)[None]
    fbias_local = jnp.stack([small_first[2], small_second[2]], 0)[None]
    sbias_local = jnp.stack([small_first[3], small_second[3]], 0)[None]
    centroid_grad, gain_grad, norm_bias_grad, in_bias_grad, out_bias_grad = lax.psum(
        (grad_centroid[None], gains_local, nbias_local, fbias_local, sbias_local), "rep"
    )
    return (
        mixed,
        tokens_grad,
        centroid_grad,
        gain_grad,
        norm_bias_grad,
        w_in_grad,
        in_bias_grad,
        w_out_grad,
        out_bias_grad,
    )


def solution(mesh):
    placed = (
        P(("rep", "exp"), None),
        P(("rep", "exp"), None),
        P(),
        P("exp", None),
        P("exp", None, None),
        P("exp", None, None),
        P("exp", None, None, "rep"),
        P("exp", None, None),
        P("exp", None, "rep", None),
        P("exp", None, None),
        P(("rep", "exp"), None),
    )
    return jax.shard_map(
        shards,
        mesh=mesh,
        in_specs=placed,
        out_specs=(
            P(("rep", "exp"), None),
            P(("rep", "exp"), None),
            P("exp", None),
            P("exp", None, None),
            P("exp", None, None),
            P("exp", None, None, "rep"),
            P("exp", None, None),
            P("exp", None, "rep", None),
            P("exp", None, None),
        ),
        check_vma=False,
    )
```

profile of v0, /device:TPU:0, one launch (start us, length us, event | category | flops | bytes accessed | tf_op | source)
XLA Modules:
  0.0 1803.3 jit_solution(14227262332793810520)
XLA Ops:
  7.3 0.7 all-gather.3.cloned.1.call-update
  8.0 0.7 all-gather.5.cloned.1.call-update
  8.8 1.1 reduce-window.6
  9.9 0.2 slice_reduce_fusion
  10.2 0.1 fusion.58
  10.3 4.2 scatter_custom_fusion
  14.5 5.2 all-to-all-start
  19.9 3.6 scatter_custom_fusion.1
  23.5 11.6 all-to-all-done
  35.1 3.6 all-to-all-start.2
  38.6 0.6 reduce-scatter.5.cloned.1.call-start
  39.2 0.5 fusion.42
  39.8 0.5 copy-done.9
  40.3 0.4 fusion.37
  40.7 13.3 all-to-all-done.2
  54.0 1.9 fusion.22
  55.9 0.4 fusion.40
  56.3 242.8 %all-gather.3.cloned.1.call-done = bf16[1,2,1024,4096]{3,2,1,0:T(8,128)(2,1)} async-done(((bf16[1,2,1024,1024]{3,2,1,0:T(8,128)(2,1)}), bf16[1,2,1024,4096]{3,2,1,0:T(8,128)(2,1)}) %all-gather.3.cloned.1.call-update) | async-done | bytes 16777232 | tf_op jit(solution)/shard_map/all_gather | solution.py:60
  299.2 10.3 fusion.13
  309.5 276.3 %all-gather.5.cloned.1.call-done = bf16[1,2,4096,1024]{3,2,1,0:T(8,128)(2,1)} async-done(((bf16[1,2,1024,1024]{3,2,1,0:T(8,128)(2,1)}), bf16[1,2,4096,1024]{3,2,1,0:T(8,128)(2,1)}) %all-gather.5.cloned.1.call-update) | async-done | bytes 16777232 | tf_op jit(solution)/shard_map/all_gather | solution.py:61
  585.7 11.3 fusion.76
  597.0 0.4 multiply_reduce_fusion.2
  597.4 10.4 fusion.17
  607.8 13.2 fusion.77
  621.1 9.7 multiply_reduce_fusion
  630.8 0.7 fusion.71
  631.5 12.7 fusion.26
  644.2 9.8 convolution_bitcast_fusion.1
  654.0 15.5 convolution_bitcast_fusion
  669.5 18.8 %maximum_bitcast_fusion.1 = f32[1,2,4096,1024]{3,2,1,0:T(8,128)} fusion(f32[1,4096,1024]{2,1,0:T(8,128)} %convolution_bitcast_fusion, f32[1,4096,1024]{2,1,0:T(8,128)S(1)} %convolution_bitcast_fusion.1), kind=kLoop, calls=%fused_computation.5 | loop fusion | flops 8388608 | bytes 67108864 | tf_op jit(solution)/shard_map/broadcast_in_dim | solution.py:117
  688.5 14.5 fusion.78
  703.1 7.3 fusion.68
  710.5 1.0 fusion.34
  711.5 2.2 fusion.36
  713.8 4.6 convolution_bitcast_fusion.3
  718.4 8.4 convolution_bitcast_fusion.2
  726.9 18.6 %maximum_bitcast_fusion = f32[1,2,1024,4096]{3,2,1,0:T(8,128)} fusion(f32[1,1024,4096]{2,1,0:T(8,128)} %convolution_bitcast_fusion.2, f32[1,1024,4096]{2,1,0:T(8,128)S(1)} %convolution_bitcast_fusion.3), kind=kLoop, calls=%fused_computation.4 | loop fusion | flops 8388608 | bytes 67108864 | tf_op jit(solution)/shard_map/broadcast_in_dim | solution.py:116
  745.5 3.7 all-to-all-start.3
  749.3 15.2 all-to-all-done.3
  764.5 3.6 all-to-all-start.1
  768.1 0.3 fusion.43
  768.5 19.6 %all-reduce = (f32[1,1024]{1,0:T(1,128)}, f32[1,2,1024]{2,1,0:T(2,128)}, f32[1,2,1024]{2,1,0:T(2,128)}, f32[1,2,4096]{2,1,0:T(2,128)}, f32[1,2,1024]{2,1,0:T(2,128)}) all-reduce(f32[1,1024]{1,0:T(1,128)S(1)} %bitcast.160, f32[1,2,1024]{2,1,0:T(2,128)S(1)} %maximum_bitcast_fusion.3, ...), channel_id=1, replica_groups=mesh['rep'=4,'exp'=8] {'rep'}, use_global_device_ids=true, to_apply=%region_17.18 | all-reduce | flops 15360 | bytes 122880 | tf_op jit(solution)/shard_map/psum | solution.py:131
  788.0 2.0 gather_fusion.1
  790.1 2.8 gather_fusion
  792.9 1.4 fusion.21
  794.3 2.9 add_convert_fusion.1
  797.2 443.6 %reduce-scatter.5.cloned.1.call-done = f32[1,2,1024,1024]{3,2,1,0:T(8,128)} async-done(((f32[1,2,4096,1024]{3,2,1,0:T(8,128)}), f32[1,2,1024,1024]{3,2,1,0:T(8,128)}) %reduce-scatter.5.cloned.1.call-update) | async-done | bytes 8388624 | tf_op jit(solution)/shard_map/reduce_scatter | solution.py:120
  1240.8 555.7 %reduce-scatter.3.cloned.1.call-done = f32[1,2,1024,1024]{3,2,1,0:T(8,128)} async-done(((f32[1,2,1024,4096]{3,2,1,0:T(8,128)}), f32[1,2,1024,1024]{3,2,1,0:T(8,128)}) %reduce-scatter.3.cloned.1.call-update) | async-done | bytes 8388624 | tf_op jit(solution)/shard_map/reduce_scatter | solution.py:119
  (86 shorter events, 0.9 us)
Async XLA Ops:
  7.2 1.6 copy-start.12
  7.2 12.5 copy-start.23
  7.2 12.6 copy-start.20
  7.2 12.6 copy-start.21
  7.2 12.6 copy-start.22
  7.2 12.6 copy-start
  7.2 16.3 copy-start.11
  7.2 32.0 %copy-start.15 = (f32[1,1024]{1,0:T(1,128)S(1)}, f32[1,1024]{1,0:T(1,128)}, u32[]{:S(2)}) copy-start(f32[1,1024]{1,0:T(1,128)} %param.14) | copy-start | bytes 12292
  7.3 291.9 %all-gather.3.cloned.1.call-start = ((), (), s32[]{:S(2)}) async-start(), calls=%async_computation.6 | async-start | bytes 20971520 | tf_op jit(solution)/shard_map/all_gather | solution.py:60
  8.0 577.7 %all-gather.5.cloned.1.call-start = ((), (), s32[]{:S(2)}) async-start(), calls=%async_computation.7 | async-start | bytes 20971520 | tf_op jit(solution)/shard_map/all_gather | solution.py:61
  10.3 30.0 %copy-start.18 = (s32[512,1]{0,1:T(1,128)}, s32[512,1]{0,1:T(1,128)S(1)}, u32[]{:S(2)}) copy-start(s32[512,1]{0,1:T(1,128)S(1)} %compare_select_fusion) | copy-start | bytes 6148
  14.5 20.6 %all-to-all-start = ((bf16[8,64,1024]{2,1,0:T(8,128)(2,1)}), bf16[8,64,1024]{2,1,0:T(8,128)(2,1)S(1)}, u32[]{:S(2)}, u32[]{:S(2)}) async-start(bf16[8,64,1024]{2,1,0:T(8,128)(2,1)} %bitcast.6), calls=%async_computation | async-start | bytes 2097152 | tf_op jit(solution)/shard_map/all_to_all | solution.py:57
  19.8 289.6 %copy-start.7 = (f32[1,1,1024]{2,1,0:T(1,128)}, f32[1,1,1024]{2,1,0:T(1,128)S(1)}, u32[]{:S(2)}) copy-start(f32[1,1,1024]{2,1,0:T(1,128)S(1)} %get-tuple-element.41) | copy-start | bytes 12292
  19.9 19.3 %copy-start.13 = (f32[512]{0:T(512)}, f32[512]{0:T(512)S(1)}, u32[]{:S(2)}) copy-start(f32[512]{0:T(512)S(1)} %fusion.63) | copy-start | bytes 6148
  35.1 18.9 %all-to-all-start.2 = ((bf16[8,64,1024]{2,1,0:T(8,128)(2,1)}), bf16[8,64,1024]{2,1,0:T(8,128)(2,1)S(1)}, u32[]{:S(2)}, u32[]{:S(2)}) async-start(bf16[8,64,1024]{2,1,0:T(8,128)(2,1)} %bitcast.24), calls=%async_computation.2 | async-start | bytes 2097152 | tf_op jit(solution)/shard_map/all_to_all | solution.py:85
  38.6 1202.2 %reduce-scatter.5.cloned.1.call-start = ((), (), s32[]{:S(2)}) async-start(), calls=%async_computation.9 | async-start | bytes 41943040 | tf_op jit(solution)/shard_map/reduce_scatter | solution.py:120
  39.7 0.6 copy-start.9
  54.0 255.5 %copy-start.2 = (bf16[8,64,1024]{2,1,0:T(8,128)(2,1)}, bf16[8,64,1024]{2,1,0:T(8,128)(2,1)S(1)}, u32[]{:S(2)}) copy-start(bf16[8,64,1024]{2,1,0:T(8,128)(2,1)S(1)} %all-to-all-done.2) | copy-start | bytes 3145732
  597.4 10.4 copy-start.6
  621.1 9.7 copy-start.24
  621.1 10.4 copy-start.3
  644.2 25.3 %copy-start.4 = (f32[512,1024]{1,0:T(8,128)}, f32[512,1024]{1,0:T(8,128)S(1)}, u32[]{:S(2)}) copy-start(f32[512,1024]{1,0:T(8,128)S(1)} %get-tuple-element.35) | copy-start | bytes 6291460
  688.3 1108.2 %reduce-scatter.3.cloned.1.call-start = ((), (), s32[]{:S(2)}) async-start(), calls=%async_computation.8 | async-start | bytes 41943040 | tf_op jit(solution)/shard_map/reduce_scatter | solution.py:119
  703.1 8.4 copy-start.5
  703.1 8.4 copy-start.8
  703.1 8.4 copy-start.16
  713.8 4.6 copy-start.25
  745.4 3.7 copy-start.19
  745.4 3.8 copy-start.17
  745.4 22.7 %copy-start.10 = (f32[8,64]{1,0:T(8,128)S(1)}, f32[8,64]{1,0:T(8,128)}, u32[]{:S(2)}) copy-start(f32[8,64]{1,0:T(8,128)} %copy-done.9) | copy-start | bytes 6148
  745.5 19.0 %all-to-all-start.3 = ((bf16[8,64,1024]{2,1,0:T(8,128)(2,1)}), bf16[8,64,1024]{2,1,0:T(8,128)(2,1)S(1)}, u32[]{:S(2)}, u32[]{:S(2)}) async-start(bf16[8,64,1024]{2,1,0:T(8,128)(2,1)} %bitcast.27), calls=%async_computation.3 | async-start | bytes 2097152 | tf_op jit(solution)/shard_map/all_to_all | solution.py:123
  764.5 25.6 %all-to-all-start.1 = ((bf16[8,64,1024]{2,1,0:T(8,128)(2,1)}), bf16[8,64,1024]{2,1,0:T(8,128)(2,1)S(1)}, u32[]{:S(2)}, u32[]{:S(2)}) async-start(bf16[8,64,1024]{2,1,0:T(8,128)(2,1)} %bitcast.145), calls=%async_computation.1 | async-start | bytes 2097152 | tf_op jit(solution)/shard_map/all_to_all | solution.py:79
  790.1 2.8 copy-start.1
  790.1 4.2 copy-start.14
Sparse Core Ops, SparseCore 0:
  9.7 289.4 all-gather.2
  300.7 284.9 all-gather.4
  688.5 552.2 reduce-scatter.4
  1243.7 552.7 reduce-scatter.2
where the time goes:
time: 1810 us; the launch traced here: 1800 us
  waiting for transfers between devices  1560 us (86%)
  matrix products  128 us (7%)
  other arithmetic  54.6 us (3%)
  blocking collectives  19.6 us (1%)
    reduce_scatter x1, waiting for transfers between devices, shards(): lax.psum_scatter(stacked_in, 'rep', scatter_dimension=3, tiled=True)  556 us
    reduce_scatter x1, waiting for transfers between devices, shards(): lax.psum_scatter(stacked_out, 'rep', scatter_dimension=2, tiled=True)  444 us
    all_gather x1, waiting for transfers between devices, shards(): lax.all_gather(w_out, 'rep', axis=2, tiled=True)  276 us
    all_gather x1, waiting for transfers between devices, shards(): lax.all_gather(w_in, 'rep', axis=3, tiled=True)  243 us
    dot_general x4, matrix products, contract_cols(): lax.dot_general(left, right, (((1,), (1,)), ((), ())), preferred_element_...  44.7 us
    dot_general x4, matrix products, contract_rows(): lax.dot_general(left, right, (((0,), (0,)), ((), ())), preferred_element_...  38.3 us
  transfers between devices with their start and end apart: 8, of which 7 were waited for; matrix products, arithmetic and copies ran while one was open for 5% of the time, Pallas kernels for 0%

commit v1 on v0

v1 whole, which is shorter than its diff:
```python
import jax
import jax.numpy as jnp
from jax import lax
from jax.sharding import PartitionSpec as P

SLOT = 2048


eps = 1e-05


def layer_norm(values, gain, bias):
    center = values - jnp.mean(values, -1, keepdims=True)
    spread = jnp.mean(center * center, -1, keepdims=True)
    return center * lax.rsqrt(spread + eps) * gain + bias


def contract_rows(left, right):
    return lax.dot_general(
        left, right, (((0,), (0,)), ((), ())), preferred_element_type=jnp.float32
    )


def contract_cols(left, right):
    return lax.dot_general(
        left, right, (((1,), (1,)), ((), ())), preferred_element_type=jnp.float32
    )


def gather_rows(values):
    return lax.all_gather(values, "rep", axis=0, tiled=True)


def scatter_rows(values):
    return lax.psum_scatter(values.astype(jnp.bfloat16), "rep", scatter_dimension=0, tiled=True).astype(
        jnp.float32
    )


def shards(
    tokens,
    routes,
    lengths,
    centroids,
    norm_gains,
    norm_biases,
    w_in,
    in_biases,
    w_out,
    out_biases,
    cotangent,
):
    n_exp = lax.axis_size("exp")
    tok_rows = tokens.shape[0]
    cap = tok_rows // n_exp
    device = lax.axis_index(("rep", "exp"))
    positions = device * tok_rows + lax.iota(jnp.int32, tok_rows)
    seq_ids = positions // SLOT
    seq_table = lax.iota(jnp.int32, lengths.shape[0])
    seq_len = jnp.sum(jnp.where(seq_ids[:, None] == seq_table[None, :], lengths[None, :], 0), 1)
    live = (positions % SLOT < seq_len).astype(jnp.float32)[:, None]
    route = routes[:, 0]
    hits = (route[:, None] == lax.iota(jnp.int32, n_exp)[None, :]).astype(jnp.int32)
    before = jnp.cumsum(hits, 0) - hits
    target = route * cap + jnp.sum(before * hits, 1)
    place = (lax.iota(jnp.int32, tok_rows)[:, None] == target[None, :]).astype(jnp.bfloat16)
    grad_out = (live * cotangent.astype(jnp.float32)).astype(jnp.bfloat16)

    def send(rows):
        ordered = jnp.dot(place, rows, preferred_element_type=jnp.float32).astype(jnp.bfloat16)
        return lax.all_to_all(ordered, "exp", split_axis=0, concat_axis=0, tiled=True)

    def give_back(rows):
        back = lax.all_to_all(rows, "exp", split_axis=0, concat_axis=0, tiled=True)
        return contract_rows(place, back)

    expert_in = send(tokens).astype(jnp.float32)
    grad_recv = send(grad_out).astype(jnp.float32)
    centroid = centroids[0]
    gate = jax.nn.sigmoid(jnp.sum(expert_in * centroid, -1))[:, None]
    grad_upper = gate * grad_recv
    ff = w_in.shape[3]
    my_bias = lax.dynamic_slice_in_dim(in_biases[0], lax.axis_index("rep") * ff, ff, 1)

    def sub_forward(values, k):
        normed = gather_rows(layer_norm(values, norm_gains[0, k], norm_biases[0, k]).astype(jnp.bfloat16))
        inner = jnp.dot(normed, w_in[0, k], preferred_element_type=jnp.float32) + my_bias[k]
        act = jax.nn.gelu(inner).astype(jnp.bfloat16)
        outer = scatter_rows(jnp.dot(act, w_out[0, k], preferred_element_type=jnp.float32))
        return (values + outer + out_biases[0, k], (values, normed, inner, act))

    middle, kept_first = sub_forward(expert_in, 0)
    upper, kept_second = sub_forward(middle, 1)
    result = (gate * upper).astype(jnp.bfloat16)
    mixed = (tokens.astype(jnp.float32) + live * give_back(result)).astype(jnp.bfloat16)
    grad_logit = jnp.sum(grad_recv * upper, -1, keepdims=True) * gate * (1.0 - gate)
    grad_centroid = jnp.sum(grad_logit * expert_in, 0)

    def sub_backward(grad_top, kept, k):
        values, normed, inner, act = kept
        grad_outer = gather_rows(grad_top.astype(jnp.bfloat16))
        grad_second = contract_rows(act, grad_outer)
        grad_sbias = jnp.sum(grad_top, 0)
        grad_act = contract_cols(grad_outer, w_out[0, k])
        grad_inner = jax.vjp(jax.nn.gelu, inner)[1](grad_act)[0]
        grad_fbias = jnp.sum(grad_inner, 0)
        grad_inner_low = grad_inner.astype(jnp.bfloat16)
        grad_first = contract_rows(normed, grad_inner_low)
        grad_normed = scatter_rows(contract_cols(grad_inner_low, w_in[0, k]))
        norm_pull = jax.vjp(layer_norm, values, norm_gains[0, k], norm_biases[0, k])[1]
        grad_values, grad_gain, grad_nbias = norm_pull(grad_normed)
        return (
            grad_top + grad_values,
            (grad_first, grad_second),
            (grad_gain, grad_nbias, grad_fbias, grad_sbias),
        )

    grad_middle, large_second, small_second = sub_backward(grad_upper, kept_second, 1)
    grad_input, large_first, small_first = sub_backward(grad_middle, kept_first, 0)
    w_in_grad = jnp.stack([large_first[0], large_second[0]], 0)[None]
    w_out_grad = jnp.stack([large_first[1], large_second[1]], 0)[None]
    grad_local = (grad_input + grad_logit * centroid).astype(jnp.bfloat16)
    tokens_grad = (cotangent.astype(jnp.float32) + give_back(grad_local)).astype(jnp.bfloat16)

    def stacked(i):
        return jnp.stack([small_first[i], small_second[i]], 0)[None]

    in_bias_grad = lax.all_gather(stacked(2), "rep", axis=2, tiled=True)
    centroid_grad, gain_grad, norm_bias_grad, out_bias_grad = lax.psum(
        (grad_centroid[None], stacked(0), stacked(1), stacked(3)), "rep"
    )
    return (
        mixed,
        tokens_grad,
        centroid_grad,
        gain_grad,
        norm_bias_grad,
        w_in_grad,
        in_bias_grad,
        w_out_grad,
        out_bias_grad,
    )


def solution(mesh):
    placed = (
        P(("rep", "exp"), None),
        P(("rep", "exp"), None),
        P(),
        P("exp", None),
        P("exp", None, None),
        P("exp", None, None),
        P("exp", None, None, "rep"),
        P("exp", None, None),
        P("exp", None, "rep", None),
        P("exp", None, None),
        P(("rep", "exp"), None),
    )
    return jax.shard_map(
        shards,
        mesh=mesh,
        in_specs=placed,
        out_specs=(
            P(("rep", "exp"), None),
            P(("rep", "exp"), None),
            P("exp", None),
            P("exp", None, None),
            P("exp", None, None),
            P("exp", None, None, "rep"),
            P("exp", None, None),
            P("exp", None, "rep", None),
            P("exp", None, None),
        ),
        check_vma=False,
    )
```

time: 1810 us -> 821 us (0.45)
  waiting for transfers between devices: 1560 us -> 570 us
    reduce_scatter x2 -> x4, waiting for transfers between devices: 999 us -> 244 us  [scatter_rows(): lax.psum_scatter(values.astype(jnp.bfloat16), 'rep', scatter_dimension=0,...]
    all_gather x2 -> x4, waiting for transfers between devices: 519 us -> 290 us  [gather_rows(): return lax.all_gather(values, 'rep', axis=0, tiled=True)]
    broadcast_in_dim x5 -> x4, other arithmetic: 37.5 us -> 9.4 us  [the longest x1 5.13 us: shards(): w_in_grad = jnp.stack([large_first[0], large_second[0]], 0)[None]]
    dot_general x4 -> x6, matrix products: 38.3 us -> 46.8 us  [contract_rows(): lax.dot_general(left, right, (((0,), (0,)), ((), ())), preferred_element_...]
    dot_general x4 -> x6, matrix products: 44.7 us -> 41.4 us  [the longest x2 18.7 us: sub_forward(): jnp.dot(act, w_out[0, k], preferred_element_type=jnp.float32)]
  transfers between devices with their start and end apart: 8 -> 12, of which waited for: 7 -> 11; matrix products, arithmetic and copies ran while one was open for 5% -> 10% of each run, Pallas kernels for 0% -> 0%
where the time goes in v1:
time: 821 us; the launch traced here: 814 us
  waiting for transfers between devices  570 us (69%)
  matrix products  129 us (16%)
  other arithmetic  37.5 us (5%)
  blocking collectives  32.2 us (4%)
  starting transfers between devices  17.4 us (2%)
  between operations  14.9 us (2%)
  local copies, waits for them, and re-layouts  12.6 us (2%)
    all_gather x4, waiting for transfers between devices, gather_rows(): return lax.all_gather(values, 'rep', axis=0, tiled=True)  290 us
    reduce_scatter x4, waiting for transfers between devices, scatter_rows(): lax.psum_scatter(values.astype(jnp.bfloat16), 'rep', scatter_dimension=0,...  244 us
    dot_general x6, matrix products, contract_rows(): lax.dot_general(left, right, (((0,), (0,)), ((), ())), preferred_element_...  46.8 us
    dot_general x4, matrix products, contract_cols(): lax.dot_general(left, right, (((1,), (1,)), ((), ())), preferred_element_...  41.2 us
    all_to_all x2, waiting for transfers between devices, send(): lax.all_to_all(ordered, 'exp', split_axis=0, concat_axis=0, tiled=True)  30.6 us
    dot_general x2, matrix products, sub_forward(): jnp.dot(act, w_out[0, k], preferred_element_type=jnp.float32)  18.7 us
    psum x1, blocking collectives, shards(): lax.psum((grad_centroid[None], stacked(0), stacked(1), stacked(3)), 'rep')  18.5 us
    dot_general x2, matrix products, sub_forward(): jnp.dot(normed, w_in[0, k], preferred_element_type=jnp.float32) + my_bias[k]  18 us
  transfers between devices with their start and end apart: 12, of which 11 were waited for; matrix products, arithmetic and copies ran while one was open for 10% of the time, Pallas kernels for 0%

profile of v1, /device:TPU:0, one launch (start us, length us, event | category | flops | bytes accessed | tf_op | source)
XLA Modules:
  0.0 813.5 jit_solution(1699933152290879380)
XLA Ops:
  10.8 2.9 convolution_convert_fusion.5
  13.7 5.2 all-to-all-start
  18.9 15.3 %all-to-all-done = bf16[8,64,1024]{2,1,0:T(8,128)(2,1)S(1)} async-done(((bf16[8,64,1024]{2,1,0:T(8,128)(2,1)}), bf16[8,64,1024]{2,1,0:T(8,128)(2,1)S(1)}, u32[]{:S(2)}, u32[]{:S(2)}) %all-to-all-start) | async-done | bytes 1048608 | tf_op jit(solution)/shard_map/all_to_all | solution.py:71
  35.3 1.4 fusion.46
  37.7 79.4 %all-gather.6.cloned.1.call-done = bf16[2048,1024]{1,0:T(8,128)(2,1)} async-done(((bf16[512,1024]{1,0:T(8,128)(2,1)}), bf16[2048,1024]{1,0:T(8,128)(2,1)}) %all-gather.6.cloned.1.call-update) | async-done | bytes 4194320 | tf_op jit(solution)/shard_map/all_gather | solution.py:31
  117.1 7.1 fusion.40
  124.2 3.4 copy-done.21
  127.5 6.9 convolution_convert_fusion.3
  135.2 74.8 %reduce-scatter.5.cloned.1.call-done = bf16[512,1024]{1,0:T(8,128)(2,1)} async-done(((bf16[2048,1024]{1,0:T(8,128)(2,1)}), bf16[512,1024]{1,0:T(8,128)(2,1)}) %reduce-scatter.5.cloned.1.call-update) | async-done | bytes 1048592 | tf_op jit(solution)/shard_map/reduce_scatter | solution.py:35
  209.9 1.8 fusion.65
  211.7 1.8 multiply_reduce_fusion
  213.5 1.6 add_convert_fusion.2
  215.3 1.8 convolution_convert_fusion.4
  217.1 3.7 all-to-all-start.2
  220.9 15.3 %all-to-all-done.2 = bf16[8,64,1024]{2,1,0:T(8,128)(2,1)S(1)} async-done(((bf16[8,64,1024]{2,1,0:T(8,128)(2,1)}), bf16[8,64,1024]{2,1,0:T(8,128)(2,1)S(1)}, u32[]{:S(2)}, u32[]{:S(2)}) %all-to-all-start.2) | async-done | bytes 1048608 | tf_op jit(solution)/shard_map/all_to_all | solution.py:71
  237.6 58.9 %all-gather.8.cloned.1.call-done = bf16[2048,1024]{1,0:T(8,128)(2,1)} async-done(((bf16[512,1024]{1,0:T(8,128)(2,1)}), bf16[2048,1024]{1,0:T(8,128)(2,1)}) %all-gather.8.cloned.1.call-update) | async-done | bytes 4194320 | tf_op jit(solution)/shard_map/all_gather | solution.py:31
  296.6 10.9 %fusion.32 = f32[2048,1024]{1,0:T(8,128)} fusion(bf16[2048,1024]{1,0:T(8,128)(2,1)} %all-gather.8.cloned.1.call-done, bf16[1,2,1024,1024]{3,2,1,0:T(8,128)(2,1)} %param.17), kind=kOutput, calls=%fused_computation.59 | convolution fusion | flops 4294967296 | bytes 14680064 | tf_op jit(solution)/shard_map/dot_general | solution.py:87
  307.5 70.5 %all-gather.10.cloned.1.call-done = bf16[2048,1024]{1,0:T(8,128)(2,1)} async-done(((bf16[512,1024]{1,0:T(8,128)(2,1)}), bf16[2048,1024]{1,0:T(8,128)(2,1)}) %all-gather.10.cloned.1.call-update) | async-done | bytes 4194320 | tf_op jit(solution)/shard_map/all_gather | solution.py:31
  378.0 14.3 %fusion.88 = (f32[1024]{0:T(1024)S(1)}, bf16[2048,1024]{1,0:T(8,128)(2,1)S(1)}) fusion(f32[2048,1024]{1,0:T(8,128)} %fusion.32, f32[1024]{0:T(1024)S(1)} %bitcast.191, bf16[2048,1024]{1,0:T(8,128)(2,1)} %all-gather.10.cloned.1.call-done, bf16[1,2,1024,1024]{3,2,1,0:T(8,128)(2,1)} %param.19), kind=kOutput, calls=%fused_computation.157 | convolution fusion | flops 4341103616 | bytes 18882560 | tf_op jit(solution)/shard_map/dot_general | solution.py:25
  392.3 2.0 copy-done.19
  394.2 6.3 convolution_convert_fusion.1
  401.0 11.8 %convolution_convert_fusion.2 = bf16[2048,1024]{1,0:T(8,128)(2,1)} fusion(bf16[1,2,1024,1024]{3,2,1,0:T(8,128)(2,1)} %param.19, f32[2048,1024]{1,0:T(8,128)} %fusion.32, f32[1024]{0:T(1024)S(1)} %bitcast.192), kind=kOutput, calls=%fused_computation.22 | convolution fusion | flops 4318035968 | bytes 14684160 | tf_op jit(solution)/shard_map/dot_general | solution.py:89
  412.8 63.2 %reduce-scatter.9.cloned.1.call-done = bf16[512,1024]{1,0:T(8,128)(2,1)} async-done(((bf16[2048,1024]{1,0:T(8,128)(2,1)}), bf16[512,1024]{1,0:T(8,128)(2,1)}) %reduce-scatter.9.cloned.1.call-update) | async-done | bytes 1048592 | tf_op jit(solution)/shard_map/reduce_scatter | solution.py:35
  476.0 2.1 convert_reduce_fusion.1
  478.1 77.3 %reduce-scatter.7.cloned.1.call-done = bf16[512,1024]{1,0:T(8,128)(2,1)} async-done(((bf16[2048,1024]{1,0:T(8,128)(2,1)}), bf16[512,1024]{1,0:T(8,128)(2,1)}) %reduce-scatter.7.cloned.1.call-update) | async-done | bytes 1048592 | tf_op jit(solution)/shard_map/reduce_scatter | solution.py:35
  555.4 4.2 fusion.20
  563.7 81.2 %all-gather.12.cloned.1.call-done = bf16[2048,1024]{1,0:T(8,128)(2,1)} async-done(((bf16[512,1024]{1,0:T(8,128)(2,1)}), bf16[2048,1024]{1,0:T(8,128)(2,1)}) %all-gather.12.cloned.1.call-update) | async-done | bytes 4194320 | tf_op jit(solution)/shard_map/all_gather | solution.py:31
  644.9 14.3 %fusion.89 = (f32[1024]{0:T(1024)S(1)}, bf16[2048,1024]{1,0:T(8,128)(2,1)S(1)}) fusion(f32[2048,1024]{1,0:T(8,128)} %copy-done.21, f32[1024]{0:T(1024)S(1)} %bitcast.189, bf16[2048,1024]{1,0:T(8,128)(2,1)} %all-gather.12.cloned.1.call-done, bf16[1,2,1024,1024]{3,2,1,0:T(8,128)(2,1)} %param.19), kind=kOutput, calls=%fused_computation.158 | convolution fusion | flops 4341103616 | bytes 18882560 | tf_op jit(solution)/shard_map/dot_general | solution.py:25
  659.2 1.9 copy-done.20
  661.1 6.3 convolution_convert_fusion
  667.7 12.8 %convolution_bitcast_fusion = f32[1,1024,1024]{2,1,0:T(8,128)} fusion(bf16[2048,1024]{1,0:T(8,128)(2,1)} %all-gather.10.cloned.1.call-done, f32[2048,1024]{1,0:T(8,128)} %fusion.32, f32[1024]{0:T(1024)S(1)} %bitcast.193), kind=kOutput, calls=%fused_computation.38 | convolution fusion | flops 4315938816 | bytes 16781312 | tf_op jit(solution)/shard_map/dot_general | solution.py:19
  680.5 3.8 all-to-all-start.1
  684.3 10.2 %convolution_bitcast_fusion.2 = f32[1,1024,1024]{2,1,0:T(8,128)} fusion(bf16[2048,1024]{1,0:T(8,128)(2,1)} %all-gather.8.cloned.1.call-done, bf16[2048,1024]{1,0:T(8,128)(2,1)} %copy-done.19), kind=kOutput, calls=%fused_computation.40 | convolution fusion | flops 4294967296 | bytes 12582912 | tf_op jit(solution)/shard_map/dot_general | solution.py:19
  694.9 4.5 all-to-all-done.1
  699.4 1.7 add_convert_fusion.1
  701.2 12.6 %convolution_bitcast_fusion.1 = f32[1,1024,1024]{2,1,0:T(8,128)} fusion(bf16[2048,1024]{1,0:T(8,128)(2,1)} %all-gather.12.cloned.1.call-done, f32[2048,1024]{1,0:T(8,128)} %copy-done.21, f32[1024]{0:T(1024)S(1)} %bitcast.190), kind=kOutput, calls=%fused_computation.39 | convolution fusion | flops 4315938816 | bytes 16781312 | tf_op jit(solution)/shard_map/dot_general | solution.py:19
  713.8 29.2 %reduce-scatter.11.cloned.1.call-done = bf16[512,1024]{1,0:T(8,128)(2,1)} async-done(((bf16[2048,1024]{1,0:T(8,128)(2,1)}), bf16[512,1024]{1,0:T(8,128)(2,1)}) %reduce-scatter.11.cloned.1.call-update) | async-done | bytes 1048592 | tf_op jit(solution)/shard_map/reduce_scatter | solution.py:35
  742.9 2.0 convert_reduce_fusion
  744.9 2.7 fusion.21
  747.6 1.9 add_convert_fusion
  749.5 3.6 all-to-all-start.3
  753.2 7.7 convolution_bitcast_fusion.3
  760.9 13.7 %all-gather = f32[2,4096]{1,0:T(2,128)S(1)} all-gather(f32[2,1024]{1,0:T(2,128)S(1)} %pad_maximum_fusion), channel_id=2, replica_groups=mesh['rep'=4,'exp'=8] {'rep'}, dimensions={1}, use_global_device_ids=true | all-gather | bytes 40960 | tf_op jit(solution)/shard_map/all_gather | solution.py:128
  774.6 5.1 maximum_bitcast_fusion
  779.7 1.4 copy-done.7
  781.1 4.2 maximum_bitcast_fusion.1
  785.4 18.5 %all-reduce = (f32[1,1024]{1,0:T(1,128)}, f32[1,2,1024]{2,1,0:T(2,128)}, f32[1,2,1024]{2,1,0:T(2,128)}, f32[1,2,1024]{2,1,0:T(2,128)}) all-reduce(f32[1,1024]{1,0:T(1,128)S(1)} %bitcast.178, f32[1,2,1024]{2,1,0:T(2,128)S(1)} %get-tuple-element.39, ...), channel_id=1, replica_groups=mesh['rep'=4,'exp'=8] {'rep'}, use_global_device_ids=true, to_apply=%region_19.20 | all-reduce | flops 7168 | bytes 57344 | tf_op jit(solution)/shard_map/psum | solution.py:129
  803.9 1.7 fusion.19
  (98 shorter events, 13.9 us)
Async XLA Ops:
  7.2 11.7 %copy-start.9 = (f32[1,2,1024]{2,1,0:T(2,128)S(1)}, f32[1,2,1024]{2,1,0:T(2,128)}, u32[]{:S(2)}) copy-start(f32[1,2,1024]{2,1,0:T(2,128)} %param.15) | copy-start | bytes 24580
  7.2 11.7 %copy-start.10 = (f32[1,2,1024]{2,1,0:T(2,128)S(1)}, f32[1,2,1024]{2,1,0:T(2,128)}, u32[]{:S(2)}) copy-start(f32[1,2,1024]{2,1,0:T(2,128)} %param.16) | copy-start | bytes 24580
  7.2 27.1 %copy-start.8 = (f32[1,1024]{1,0:T(1,128)S(1)}, f32[1,1024]{1,0:T(1,128)}, u32[]{:S(2)}) copy-start(f32[1,1024]{1,0:T(1,128)} %param.14) | copy-start | bytes 12292
  13.7 20.6 %all-to-all-start = ((bf16[8,64,1024]{2,1,0:T(8,128)(2,1)}), bf16[8,64,1024]{2,1,0:T(8,128)(2,1)S(1)}, u32[]{:S(2)}, u32[]{:S(2)}) async-start(bf16[8,64,1024]{2,1,0:T(8,128)(2,1)} %bitcast.4), calls=%async_computation | async-start | bytes 2097152 | tf_op jit(solution)/shard_map/all_to_all | solution.py:71
  18.8 98.2 %all-gather.6.cloned.1.call-start = ((), (), s32[]{:S(2)}) async-start(), calls=%async_computation.8 | async-start | bytes 5242880 | tf_op jit(solution)/shard_map/all_gather | solution.py:31
  36.8 173.2 %reduce-scatter.5.cloned.1.call-start = ((), (), s32[]{:S(2)}) async-start(), calls=%async_computation.9 | async-start | bytes 5242880 | tf_op jit(solution)/shard_map/reduce_scatter | solution.py:35
  117.1 10.5 %copy-start.13 = (bf16[1,2,1024,1024]{3,2,1,0:T(8,128)(2,1)S(1)}, bf16[1,2,1024,1024]{3,2,1,0:T(8,128)(2,1)}, u32[]{:S(2)}) copy-start(bf16[1,2,1024,1024]{3,2,1,0:T(8,128)(2,1)} %param.19) | copy-start | bytes 12582916
  124.1 3.4 copy-start.21
  134.5 0.7 copy-start.11
  134.5 162.1 %all-gather.8.cloned.1.call-start = ((), (), s32[]{:S(2)}) async-start(), calls=%async_computation.10 | async-start | bytes 5242880 | tf_op jit(solution)/shard_map/all_gather | solution.py:31
  209.9 3.6 copy-start
  209.9 5.2 copy-start.12
  209.9 5.3 copy-start.17
  217.1 19.1 %all-to-all-start.2 = ((bf16[8,64,1024]{2,1,0:T(8,128)(2,1)}), bf16[8,64,1024]{2,1,0:T(8,128)(2,1)S(1)}, u32[]{:S(2)}, u32[]{:S(2)}) async-start(bf16[8,64,1024]{2,1,0:T(8,128)(2,1)} %bitcast.157), calls=%async_computation.4 | async-start | bytes 2097152 | tf_op jit(solution)/shard_map/all_to_all | solution.py:71
  220.7 157.2 %all-gather.10.cloned.1.call-start = ((), (), s32[]{:S(2)}) async-start(), calls=%async_computation.12 | async-start | bytes 5242880 | tf_op jit(solution)/shard_map/all_gather | solution.py:31
  237.4 238.6 %reduce-scatter.9.cloned.1.call-start = ((), (), s32[]{:S(2)}) async-start(), calls=%async_computation.13 | async-start | bytes 5242880 | tf_op jit(solution)/shard_map/reduce_scatter | solution.py:35
  378.0 16.3 %copy-start.14 = (bf16[1,2,1024,1024]{3,2,1,0:T(8,128)(2,1)S(1)}, bf16[1,2,1024,1024]{3,2,1,0:T(8,128)(2,1)}, u32[]{:S(2)}) copy-start(bf16[1,2,1024,1024]{3,2,1,0:T(8,128)(2,1)} %param.17) | copy-start | bytes 12582916
  392.3 2.0 copy-start.19
  400.5 154.9 %reduce-scatter.7.cloned.1.call-start = ((), (), s32[]{:S(2)}) async-start(), calls=%async_computation.11 | async-start | bytes 5242880 | tf_op jit(solution)/shard_map/reduce_scatter | solution.py:35
  412.8 232.1 %all-gather.12.cloned.1.call-start = ((), (), s32[]{:S(2)}) async-start(), calls=%async_computation.14 | async-start | bytes 5242880 | tf_op jit(solution)/shard_map/all_gather | solution.py:31
  555.4 4.3 copy-start.4
  561.0 1.3 copy-start.1
  563.5 179.4 %reduce-scatter.11.cloned.1.call-start = ((), (), s32[]{:S(2)}) async-start(), calls=%async_computation.15 | async-start | bytes 5242880 | tf_op jit(solution)/shard_map/reduce_scatter | solution.py:35
  644.9 16.2 %copy-start.15 = (bf16[1,2,1024,1024]{3,2,1,0:T(8,128)(2,1)S(1)}, bf16[1,2,1024,1024]{3,2,1,0:T(8,128)(2,1)}, u32[]{:S(2)}) copy-start(bf16[1,2,1024,1024]{3,2,1,0:T(8,128)(2,1)} %param.17) | copy-start | bytes 12582916
  659.2 1.9 copy-start.20
  680.5 18.9 %all-to-all-start.1 = ((bf16[8,64,1024]{2,1,0:T(8,128)(2,1)}), bf16[8,64,1024]{2,1,0:T(8,128)(2,1)S(1)}, u32[]{:S(2)}, u32[]{:S(2)}) async-start(bf16[8,64,1024]{2,1,0:T(8,128)(2,1)} %bitcast.19), calls=%async_computation.3 | async-start | bytes 2097152 | tf_op jit(solution)/shard_map/all_to_all | solution.py:74
  684.3 15.1 %copy-start.16 = (bf16[512,1024]{1,0:T(8,128)(2,1)S(1)}, bf16[512,1024]{1,0:T(8,128)(2,1)}, u32[]{:S(2)}) copy-start(bf16[512,1024]{1,0:T(8,128)(2,1)} %param.11) | copy-start | bytes 3145732
  713.8 33.9 %copy-start.2 = (f32[512,1024]{1,0:T(8,128)S(1)}, f32[512,1024]{1,0:T(8,128)}, u32[]{:S(2)}) copy-start(f32[512,1024]{1,0:T(8,128)} %copy-done.1) | copy-start | bytes 6291460
  742.9 4.7 copy-start.3
  749.5 54.4 %all-to-all-start.3 = ((bf16[8,64,1024]{2,1,0:T(8,128)(2,1)}), bf16[8,64,1024]{2,1,0:T(8,128)(2,1)S(1)}, u32[]{:S(2)}, u32[]{:S(2)}) async-start(bf16[8,64,1024]{2,1,0:T(8,128)(2,1)} %bitcast.154), calls=%async_computation.7 | async-start | bytes 2097152 | tf_op jit(solution)/shard_map/all_to_all | solution.py:74
  753.2 21.5 %copy-start.6 = (f32[1,1024,1024]{2,1,0:T(8,128)S(1)}, f32[1,1024,1024]{2,1,0:T(8,128)}, u32[]{:S(2)}) copy-start(f32[1,1024,1024]{2,1,0:T(8,128)} %convolution_bitcast_fusion.2) | copy-start | bytes 12582916
  774.6 5.1 copy-start.5
  774.6 6.5 copy-start.7
  781.1 22.8 %copy-start.18 = (bf16[512,1024]{1,0:T(8,128)(2,1)S(1)}, bf16[512,1024]{1,0:T(8,128)(2,1)}, u32[]{:S(2)}) copy-start(bf16[512,1024]{1,0:T(8,128)(2,1)} %param.21) | copy-start | bytes 3145732
Sparse Core Ops, SparseCore 0:
  36.9 80.1 all-gather.5
  134.6 75.2 reduce-scatter.4
  215.2 81.2 all-gather.7
  298.6 79.2 all-gather.9
  400.7 75.2 reduce-scatter.8
  478.1 77.2 reduce-scatter.6
  563.6 81.2 all-gather.11
  667.6 75.2 reduce-scatter.10

commit v2 on v1

v2 whole, which is shorter than its diff:
```python
import functools

import jax
import jax.numpy as jnp
from jax import lax
from jax.experimental import pallas as pl
from jax.experimental.pallas import tpu as pltpu
from jax.sharding import PartitionSpec as P

SLOT = 2048


eps = 1e-05
VMEM_BYTES = 60 * 1024 * 1024


def contract_rows(left, right):
    return lax.dot_general(
        left, right, (((0,), (0,)), ((), ())), preferred_element_type=jnp.float32
    )


def contract_cols(left, right):
    return lax.dot_general(
        left, right, (((1,), (1,)), ((), ())), preferred_element_type=jnp.float32
    )


MESH = pl.DeviceIdType.MESH
CHUNKS = 4
POOL = 4
ROOT = 0.7978845608028654
CUBE = 0.044715


def layer_stats(values):
    center = values - jnp.mean(values, -1, keepdims=True)
    spread = jnp.mean(center * center, -1, keepdims=True)
    scale = lax.rsqrt(spread + eps)
    return center * scale, scale


def gelu_and_slope(inner):
    square = inner * inner
    bent = jnp.tanh(inner * (ROOT + (ROOT * CUBE) * square))
    half = 0.5 * (1.0 + bent)
    slope = half + (0.5 * inner) * (1.0 - bent * bent) * (ROOT + (3.0 * ROOT * CUBE) * square)
    return inner * half, slope


def fold(rows):
    return jnp.sum(rows.reshape(rows.shape[0] // 8, 8, rows.shape[1]), 0)


def kernel(
    n,
    x_ref,
    dy_ref,
    gain_ref,
    nbias_ref,
    cent_ref,
    bin_ref,
    bout_ref,
    wi_hbm,
    wo_hbm,
    y_ref,
    dv_ref,
    gwi_hbm,
    gwo_hbm,
    sums_ref,
    bins_ref,
    gath,
    wi,
    wo,
    gwi,
    gwo,
    part,
    act,
    dq,
    slope,
    total,
    state,
    dlog,
    recv,
    stage,
    accs,
    bacc,
    mine,
    peers,
    send_sem,
    recv_sem,
    load_sem,
    store_sem,
    peer_send,
    peer_recv,
):
    r = lax.axis_index("rep")
    rows, width = x_ref.shape
    hidden = bin_ref.shape[1]
    chunk = rows // CHUNKS
    half = chunk // 2
    ops = 4 * CHUNKS
    rounds = ops + 1
    block = min(32, chunk)
    tile = min(512, hidden)
    wtile = hidden // 4
    last = n - 1

    def op_type(i):
        return jnp.where(i < CHUNKS, 0, jnp.where(i >= 3 * CHUNKS, 3, 1 + lax.rem(i + CHUNKS, 2)))

    def op_chunk(i):
        return jnp.where(
            i < CHUNKS, i, jnp.where(i >= 3 * CHUNKS, i - 3 * CHUNKS, (i - CHUNKS) // 2)
        )

    def op_slot(i):
        return jnp.where(i < CHUNKS, i, CHUNKS + lax.rem(i, POOL))

    def half_rows(h):
        return pl.ds(h * half, half)

    ahead = (jnp.minimum(r + 1, last), jnp.maximum(r - 1, 0))
    pos = (r, last - r)

    def item_sent(d, s):
        return lax.rem(r - s + n, n) if d == 0 else lax.rem(r + s, n)

    def sends(d, k, s):
        return (pos[d] < last) & jnp.where(s <= pos[d], k < ops, k >= 1)

    def receives(d, k, s):
        return (pos[d] > 0) & jnp.where(s <= pos[d] - 1, k < ops, k >= 1)

    def copy(d, k, s, h, src, dst):
        return pltpu.make_async_remote_copy(
            src_ref=src,
            dst_ref=dst,
            send_sem=send_sem.at[d, lax.rem(s, 2), h],
            recv_sem=recv_sem.at[d, lax.rem(k, 2), s, h],
            device_id={"rep": ahead[d]},
            device_id_type=MESH,
        )

    def landing(d, k, s, h):
        return recv.at[d, lax.rem(k, 2), s, h]

    def wait_sent(d, k, s, h):
        @pl.when(sends(d, k, s))
        def _():
            copy(d, k, s, h, stage.at[d, lax.rem(s, 2), h], landing(d, k, s, h)).wait_send()

    def wait_received(d, k, s, h):
        @pl.when(receives(d, k, s))
        def _():
            copy(d, k, s, h, stage.at[d, lax.rem(s, 2), h], landing(d, k, s, h)).wait_recv()

    def finish_sum(k, h):
        rs = half_rows(h)
        total[rs, :] = part[r, rs, :]
        for d in range(2):

            @pl.when(pos[d] > 0)
            def _():
                total[rs, :] += landing(d, k, n - 1, h)[...].astype(jnp.float32)

    def send(d, k, s, h):
        gathers = s <= pos[d]
        p = item_sent(d, s)
        rs = half_rows(h)

        @pl.when(sends(d, k, s) & gathers)
        def _():
            here = gath.at[op_slot(k), p, rs]
            copy(d, k, s, h, here, here).start()

        @pl.when(sends(d, k, s) & jnp.logical_not(gathers))
        def _():
            out = stage.at[d, lax.rem(s, 2), h]

            @pl.when(pos[d] == 0)
            def _():
                out[...] = part[p, rs, :].astype(jnp.bfloat16)

            @pl.when(pos[d] > 0)
            def _():
                came = landing(d, k, s - 1, h)[...].astype(jnp.float32)
                out[...] = (part[p, rs, :] + came).astype(jnp.bfloat16)

            copy(d, k, s, h, out, landing(d, k, s, h)).start()

    def over_blocks(body):
        def step(b, carry):
            body(pl.multiple_of(b * block, block))
            return carry

        lax.fori_loop(0, chunk // block, step, 0)

    def gate_of(x):
        return jax.nn.sigmoid(jnp.sum(x * cent_ref[...], -1, keepdims=True))

    def prepare(i):
        kind, c, slot = op_type(i), op_chunk(i), op_slot(i)

        def own(offset, value):
            gath[slot, r, pl.ds(offset, block), :] = value.astype(jnp.bfloat16)

        def source(offset):
            return pl.ds(pl.multiple_of(c * chunk + offset, block), block)

        @pl.when(kind == 0)
        def _():
            over_blocks(
                lambda o: own(
                    o,
                    layer_stats(x_ref[source(o), :].astype(jnp.float32))[0] * gain_ref[0:1, :]
                    + nbias_ref[0:1, :],
                )
            )

        @pl.when(kind == 1)
        def _():
            over_blocks(
                lambda o: own(
                    o, layer_stats(state[source(o), :])[0] * gain_ref[1:2, :] + nbias_ref[1:2, :]
                )
            )

        @pl.when(kind == 2)
        def _():
            over_blocks(
                lambda o: own(
                    o,
                    gate_of(x_ref[source(o), :].astype(jnp.float32))
                    * dy_ref[source(o), :].astype(jnp.float32),
                )
            )

        @pl.when(kind == 3)
        def _():
            over_blocks(lambda o: own(o, state[source(o), :]))

    def norm_back(values, grad, k):
        unit, scale = layer_stats(values)
        accs[1 + k] += fold(grad * unit)
        accs[3 + k] += fold(grad)
        through = grad * gain_ref[k : k + 1, :]
        return scale * (
            through
            - jnp.mean(through, -1, keepdims=True)
            - unit * jnp.mean(through * unit, -1, keepdims=True)
        )

    def finish(i):
        kind, c = op_type(i), op_chunk(i)

        def source(offset):
            return pl.ds(pl.multiple_of(c * chunk + offset, block), block)

        @pl.when(kind == 0)
        def _():
            def body(o):
                state[source(o), :] = (
                    x_ref[source(o), :].astype(jnp.float32)
                    + total[pl.ds(o, block), :]
                    + bout_ref[0:1, :]
                )

            over_blocks(body)

        @pl.when(kind == 1)
        def _():
            def body(o):
                x = x_ref[source(o), :].astype(jnp.float32)
                dy = dy_ref[source(o), :].astype(jnp.float32)
                upper = state[source(o), :] + total[pl.ds(o, block), :] + bout_ref[1:2, :]
                gate = gate_of(x)
                y_ref[source(o), :] = (gate * upper).astype(jnp.bfloat16)
                logit = jnp.sum(dy * upper, -1, keepdims=True) * gate * (1.0 - gate)
                dlog[source(o), :] = jnp.broadcast_to(logit, (block, dlog.shape[1]))
                accs[0] += fold(logit * x)

            over_blocks(body)

        @pl.when(kind == 2)
        def _():
            def body(o):
                x = x_ref[source(o), :].astype(jnp.float32)
                top = gate_of(x) * dy_ref[source(o), :].astype(jnp.float32)
                middle = top + norm_back(state[source(o), :], total[pl.ds(o, block), :], 1)
                state[source(o), :] = middle
                accs[5] += fold(middle)
                accs[6] += fold(top)

            over_blocks(body)

        @pl.when(kind == 3)
        def _():
            def body(o):
                x = x_ref[source(o), :].astype(jnp.float32)
                dv_ref[source(o), :] = (
                    state[source(o), :]
                    + norm_back(x, total[pl.ds(o, block), :], 0)
                    + dlog[source(o), 0:1] * cent_ref[...]
                ).astype(jnp.bfloat16)

            over_blocks(body)

    def over_tiles(count, size, body):
        def step(j, carry):
            body(pl.ds(pl.multiple_of(j * size, size), size))
            return carry

        lax.fori_loop(0, count, step, 0)

    def item_first(i, par, p):
        kind = op_type(i)
        k = jnp.where((kind == 1) | (kind == 2), 1, 0)
        slot = jnp.where(
            kind == 2, op_slot(i - 1), jnp.where(kind == 3, op_chunk(i), op_slot(i))
        )

        def body(cs):
            inner = (
                jnp.dot(gath[slot, p], wi[k, :, cs], preferred_element_type=jnp.float32)
                + bin_ref[pl.ds(k, 1), cs]
            )
            low, pull = gelu_and_slope(inner)
            act[par, p, :, cs] = low.astype(jnp.bfloat16)
            slope[:, cs] = pull

        over_tiles(hidden // tile, tile, body)

    def item_second(i, par, p):
        kind = op_type(i)
        k = jnp.where((kind == 1) | (kind == 2), 1, 0)

        @pl.when(kind < 2)
        def _():
            def body(cs):
                part[p, :, cs] = jnp.dot(
                    act[par, p], wo[k, :, cs], preferred_element_type=jnp.float32
                )

            over_tiles(width // tile, tile, body)

        @pl.when(kind >= 2)
        def _():
            slot = op_slot(i)

            def pull(cs):
                grad = contract_cols(gath[slot, p], wo[k, cs, :]) * slope[:, cs]
                bacc[k, :, cs] += fold(grad)
                dq[par, p, :, cs] = grad.astype(jnp.bfloat16)

            over_tiles(hidden // tile, tile, pull)

            def push(cs):
                part[p, :, cs] = contract_cols(dq[par, p], wi[k, cs, :])

            over_tiles(width // tile, tile, push)

    def weight_grads(i, par, j):
        kind = op_type(i)
        k = jnp.where(kind == 2, 1, 0)
        slot = jnp.where(kind == 2, op_slot(i - 1), op_chunk(i))
        cs = pl.ds(pl.multiple_of(j * wtile, wtile), wtile)
        depth = n * chunk
        normed = gath[slot, :, :, cs].reshape(depth, wtile)
        gwi[k, cs, :] += contract_rows(normed, dq[par].reshape(depth, hidden))
        active = act[par, :, :, cs].reshape(depth, wtile)
        gwo[k, cs, :] += contract_rows(active, gath[op_slot(i)].reshape(depth, width))

    def item_at(s):
        near = jnp.minimum(r, last - r)
        base = jnp.where(near == 0, last - s, jnp.where(s < 2, last - s, s - 2))
        return jnp.where(r < 2, base, last - base)

    def load(w):
        src, dst = ((wi_hbm, wi), (wo_hbm, wo))[w]
        return pltpu.make_async_copy(src, dst, load_sem.at[w])

    def store(w, k):
        src, dst = ((gwi, gwi_hbm), (gwo, gwo_hbm))[w]
        return pltpu.make_async_copy(src.at[k], dst.at[k], store_sem.at[w, k])

    barrier = pltpu.get_barrier_semaphore()
    for q in range(1, n):
        pl.semaphore_signal(
            barrier, inc=1, device_id={"rep": lax.rem(r + q, n)}, device_id_type=MESH
        )
    load(0).start()
    load(1).start()
    prepare(0)
    pl.semaphore_wait(barrier, n - 1)

    def step(t, carry):
        k, s = t // n, lax.rem(t, n)
        k_before, s_before = (t - 1) // n, lax.rem(t + n - 1, n)
        i = k - 1
        par = lax.rem(k, 2)
        p = item_at(s)

        def exchange(h):
            for d in range(2):

                @pl.when(t >= 1)
                def _():
                    wait_received(d, k_before, s_before, h)

                @pl.when(t >= 2)
                def _():
                    wait_sent(d, (t - 2) // n, lax.rem(t + n - 2, n), h)

            @pl.when((s == 0) & (k >= 2))
            def _():
                finish_sum(k - 1, h)

            for d in range(2):
                send(d, k, s, h)

        def grads(j):
            old = k - 2

            @pl.when((s < 2) & (old >= CHUNKS) & (op_type(old) >= 2))
            def _():
                weight_grads(old, lax.rem(k + 1, 2), j)

        exchange(0)

        @pl.when(t == 0)
        def _():
            def clear(b, carry):
                zero_rows = pl.ds(pl.multiple_of(b * 64, 64), 64)
                for w in range(2):
                    gwi[w, zero_rows, :] = jnp.zeros((64, hidden), jnp.float32)
                    gwo[w, zero_rows, :] = jnp.zeros((64, width), jnp.float32)
                return carry

            lax.fori_loop(0, width // 64, clear, 0)
            accs[...] = jnp.zeros_like(accs)
            bacc[...] = jnp.zeros_like(bacc)

        @pl.when(t == n)
        def _():
            load(0).wait()
            load(1).wait()

        @pl.when(k >= 1)
        def _():
            item_first(i, par, p)

        grads(2 * s)
        exchange(1)

        @pl.when(k >= 1)
        def _():
            item_second(i, par, p)

        grads(2 * s + 1)

        @pl.when((s == 2) & (k >= 2))
        def _():
            finish(k - 2)

        @pl.when((s == 3) & (k < ops - 1))
        def _():
            prepare(k + 1)

        @pl.when(t == n * (3 * CHUNKS + 1) + 2)
        def _():
            store(0, 1).start()
            store(1, 1).start()

        return carry

    steps = rounds * n
    lax.fori_loop(0, steps, step, 0)

    def last_grads(j, carry):
        weight_grads(ops - 1, (rounds - 1) % 2, j)
        return carry

    lax.fori_loop(0, 4, last_grads, 0)
    store(0, 0).start()
    store(1, 0).start()
    for h in range(2):
        for d in range(2):
            wait_received(d, rounds - 1, n - 1, h)
        finish_sum(rounds - 1, h)
    finish(ops - 1)
    for h in range(2):
        for d in range(2):
            for back in (2, 1):
                wait_sent(d, (steps - back) // n, (steps - back) % n, h)

    for a in range(7):
        mine[a : a + 1, :width] = jnp.sum(accs[a], 0, keepdims=True)
    mine[7:8, :] = jnp.zeros((1, mine.shape[1]), jnp.float32)
    for k in range(2):
        mine[8 + k : 9 + k, :hidden] = jnp.sum(bacc[k], 0, keepdims=True)
    mine[10:16, :] = jnp.zeros((6, mine.shape[1]), jnp.float32)

    def tell(q):
        return pltpu.make_async_remote_copy(
            src_ref=mine,
            dst_ref=peers.at[q - 1],
            send_sem=peer_send.at[q - 1],
            recv_sem=peer_recv.at[q - 1],
            device_id={"rep": lax.rem(r + q, n)},
            device_id_type=MESH,
        )

    for q in range(1, n):
        tell(q).start()
    sums = mine[0:8, :width]
    bins_ref[r] = mine[8:16, :hidden]
    for q in range(1, n):
        tell(q).wait_recv()
        sums += peers[q - 1, 0:8, :width]
        bins_ref[lax.rem(r - q + n, n)] = peers[q - 1, 8:16, :hidden]
    sums_ref[...] = sums
    for q in range(1, n):
        tell(q).wait_send()
    for w in range(2):
        for k in range(2):
            store(w, k).wait()


def run_layer(x, dy, gains, nbias, cent, my_bias, bout, wi, wo):
    n = lax.axis_size("rep")
    rows, width = x.shape
    hidden = wi.shape[2]
    chunk = rows // CHUNKS
    half = chunk // 2
    wide = max(width, hidden)
    low, full = jnp.bfloat16, jnp.float32
    vmem = pl.BlockSpec(memory_space=pltpu.VMEM)
    anywhere = pl.BlockSpec(memory_space=pl.ANY)
    flops = 2 * 16 * n * rows * width * hidden
    return pl.pallas_call(
        functools.partial(kernel, n),
        out_shape=(
            jax.ShapeDtypeStruct((rows, width), low),
            jax.ShapeDtypeStruct((rows, width), low),
            jax.ShapeDtypeStruct((2, width, hidden), full),
            jax.ShapeDtypeStruct((2, hidden, width), full),
            jax.ShapeDtypeStruct((8, width), full),
            jax.ShapeDtypeStruct((n, 8, hidden), full),
        ),
        in_specs=[vmem] * 7 + [anywhere] * 2,
        out_specs=(vmem, vmem, anywhere, anywhere, vmem, vmem),
        scratch_shapes=[
            pltpu.VMEM((CHUNKS + POOL, n, chunk, width), low),
            pltpu.VMEM((2, width, hidden), low),
            pltpu.VMEM((2, hidden, width), low),
            pltpu.VMEM((2, width, hidden), full),
            pltpu.VMEM((2, hidden, width), full),
            pltpu.VMEM((n, chunk, width), full),
            pltpu.VMEM((2, n, chunk, hidden), low),
            pltpu.VMEM((2, n, chunk, hidden), low),
            pltpu.VMEM((chunk, hidden), full),
            pltpu.VMEM((chunk, width), full),
            pltpu.VMEM((rows, width), full),
            pltpu.VMEM((rows, 128), full),
            pltpu.VMEM((2, 2, n, 2, half, width), low),
            pltpu.VMEM((2, 2, 2, half, width), low),
            pltpu.VMEM((7, 8, width), full),
            pltpu.VMEM((2, 8, hidden), full),
            pltpu.VMEM((16, wide), full),
            pltpu.VMEM((n - 1, 16, wide), full),
            pltpu.SemaphoreType.DMA((2, 2, 2)),
            pltpu.SemaphoreType.DMA((2, 2, n, 2)),
            pltpu.SemaphoreType.DMA((2,)),
            pltpu.SemaphoreType.DMA((2, 2)),
            pltpu.SemaphoreType.DMA((n - 1,)),
            pltpu.SemaphoreType.DMA((n - 1,)),
        ],
        compiler_params=pltpu.CompilerParams(
            collective_id=0, has_side_effects=True, vmem_limit_bytes=VMEM_BYTES
        ),
        cost_estimate=pl.CostEstimate(
            flops=flops, bytes_accessed=40 * rows * width, transcendentals=8 * rows * hidden * n
        ),
    )(x, dy, gains, nbias, cent, my_bias, bout, wi, wo)


def shards(
    tokens,
    routes,
    lengths,
    centroids,
    norm_gains,
    norm_biases,
    w_in,
    in_biases,
    w_out,
    out_biases,
    cotangent,
):
    n_exp = lax.axis_size("exp")
    tok_rows = tokens.shape[0]
    cap = tok_rows // n_exp
    device = lax.axis_index(("rep", "exp"))
    positions = device * tok_rows + lax.iota(jnp.int32, tok_rows)
    seq_ids = positions // SLOT
    seq_table = lax.iota(jnp.int32, lengths.shape[0])
    seq_len = jnp.sum(jnp.where(seq_ids[:, None] == seq_table[None, :], lengths[None, :], 0), 1)
    live = (positions % SLOT < seq_len).astype(jnp.float32)[:, None]
    route = routes[:, 0]
    hits = (route[:, None] == lax.iota(jnp.int32, n_exp)[None, :]).astype(jnp.int32)
    before = jnp.cumsum(hits, 0) - hits
    target = route * cap + jnp.sum(before * hits, 1)
    place = (lax.iota(jnp.int32, tok_rows)[:, None] == target[None, :]).astype(jnp.bfloat16)
    grad_out = (live * cotangent.astype(jnp.float32)).astype(jnp.bfloat16)

    def send(rows):
        ordered = jnp.dot(place, rows, preferred_element_type=jnp.float32).astype(jnp.bfloat16)
        return lax.all_to_all(ordered, "exp", split_axis=0, concat_axis=0, tiled=True)

    def give_back(rows):
        back = lax.all_to_all(rows, "exp", split_axis=0, concat_axis=0, tiled=True)
        return contract_rows(place, back)

    ff = w_in.shape[3]
    my_bias = lax.dynamic_slice_in_dim(in_biases[0], lax.axis_index("rep") * ff, ff, 1)
    result, grad_local, w_in_grad, w_out_grad, sums, bins = run_layer(
        send(tokens),
        send(grad_out),
        norm_gains[0],
        norm_biases[0],
        centroids,
        my_bias,
        out_biases[0],
        w_in[0],
        w_out[0],
    )
    mixed = (tokens.astype(jnp.float32) + live * give_back(result)).astype(jnp.bfloat16)
    tokens_grad = (cotangent.astype(jnp.float32) + give_back(grad_local)).astype(jnp.bfloat16)
    in_bias_grad = jnp.transpose(bins[:, 0:2], (1, 0, 2)).reshape(1, 2, -1)
    return (
        mixed,
        tokens_grad,
        sums[0:1],
        sums[1:3][None],
        sums[3:5][None],
        w_in_grad[None],
        in_bias_grad,
        w_out_grad[None],
        sums[5:7][None],
    )


def solution(mesh):
    placed = (
        P(("rep", "exp"), None),
        P(("rep", "exp"), None),
        P(),
        P("exp", None),
        P("exp", None, None),
        P("exp", None, None),
        P("exp", None, None, "rep"),
        P("exp", None, None),
        P("exp", None, "rep", None),
        P("exp", None, None),
        P(("rep", "exp"), None),
    )
    return jax.shard_map(
        shards,
        mesh=mesh,
        in_specs=placed,
        out_specs=(
            P(("rep", "exp"), None),
            P(("rep", "exp"), None),
            P("exp", None),
            P("exp", None, None),
            P("exp", None, None),
            P("exp", None, None, "rep"),
            P("exp", None, None),
            P("exp", None, "rep", None),
            P("exp", None, None),
        ),
        check_vma=False,
    )
```

time: 821 us -> 493 us (0.60)
  waiting for transfers between devices: 570 us -> 39.3 us
  Pallas kernels: 0 us -> 391 us
  matrix products: 129 us -> 9.63 us
  other arithmetic: 37.5 us -> 4.08 us
  between operations: 14.9 us -> 0.74 us
  blocking collectives: 32.2 us -> 19.7 us
    pallas_call x0 -> x1, Pallas kernels: none -> 391 us  [run_layer(): pl.pallas_call(functools.partial(kernel, n), out_shape=(jax.ShapeDtypeStr...]
    all_gather x4 -> x0, waiting for transfers between devices: 290 us -> none  [gather_rows(): return lax.all_gather(values, 'rep', axis=0, tiled=True)]
    reduce_scatter x4 -> x0, waiting for transfers between devices: 244 us -> none  [scatter_rows(): lax.psum_scatter(values.astype(jnp.bfloat16), 'rep', scatter_dimension=0,...]
    dot_general x8 -> x0, matrix products: 77.8 us -> none  [the longest x4 41.2 us: contract_cols(): lax.dot_general(left, right, (((1,), (1,)), ((), ())), preferred_element_...]
    dot_general x6 -> x2, matrix products: 46.8 us -> 4.84 us  [contract_rows(): lax.dot_general(left, right, (((0,), (0,)), ((), ())), preferred_element_...]
    all_to_all x0 -> x1, blocking collectives: none -> 19.7 us  [give_back(): back = lax.all_to_all(rows, 'exp', split_axis=0, concat_axis=0, tiled=True)]
    psum x1 -> x0, blocking collectives: 18.5 us -> none  [shards(): lax.psum((grad_centroid[None], stacked(0), stacked(1), stacked(3)), 'rep')]
    reduce_sum x11 -> x0, other arithmetic: 17.3 us -> none  [the longest x4 11 us: layer_norm(): return center * lax.rsqrt(spread + eps) * gain + bias]
  transfers between devices with their start and end apart: 12 -> 3, of which waited for: 11 -> 3; matrix products, arithmetic and copies ran while one was open for 10% -> 1% of each run, Pallas kernels for 0% -> 0%
where the time goes in v2:
time: 493 us
  Pallas kernels  391 us (79%)
  waiting for transfers between devices  39.3 us (8%)
  blocking collectives  19.7 us (4%)
  local copies, waits for them, and re-layouts  16.5 us (3%)
  starting transfers between devices  12.3 us (2%)
  matrix products  9.63 us (2%)
    pallas_call x1, Pallas kernels, run_layer(): pl.pallas_call(functools.partial(kernel, n), out_shape=(jax.ShapeDtypeStr...  391 us
    all_to_all x2, waiting for transfers between devices, send(): lax.all_to_all(ordered, 'exp', split_axis=0, concat_axis=0, tiled=True)  28.4 us
    all_to_all x1, blocking collectives, give_back(): back = lax.all_to_all(rows, 'exp', split_axis=0, concat_axis=0, tiled=True)  19.7 us
    unnamed x18, local copies, waits for them, and re-layouts  13 us
    all_to_all x1, waiting for transfers between devices, give_back(): back = lax.all_to_all(rows, 'exp', split_axis=0, concat_axis=0, tiled=True)  10.9 us
  transfers between devices with their start and end apart: 3, of which 3 were waited for; matrix products, arithmetic and copies ran while one was open for 1% of the time, Pallas kernels for 0%

profile of v2, /device:TPU:0, one launch (start us, length us, event | category | flops | bytes accessed | tf_op | source)
XLA Modules:
  0.0 492.9 jit_solution(17969522328017689443)
XLA Ops:
  0.6 0.0 copy-start
  0.7 0.7 select_reduce_fusion
  1.4 0.7 fusion.10
  2.1 1.1 reduce-window.6
  3.3 0.2 slice_reduce_fusion
  3.5 0.8 fusion.9
  4.3 0.7 multiply_add_fusion
  5.0 0.0 copy-start.5
  5.0 3.1 convolution_convert_fusion
  8.1 5.2 %all-to-all-start.1 = ((bf16[8,64,1024]{2,1,0:T(8,128)(2,1)}), bf16[8,64,1024]{2,1,0:T(8,128)(2,1)S(1)}, u32[]{:S(2)}, u32[]{:S(2)}) async-start(bf16[8,64,1024]{2,1,0:T(8,128)(2,1)} %bitcast.6), calls=%async_computation.1 | async-start | bytes 2097152 | tf_op jit(solution)/shard_map/all_to_all | solution.py:619
  13.2 0.0 copy-done.5
  13.2 1.7 convolution_convert_fusion.1
  14.9 13.7 %all-to-all-done.1 = bf16[8,64,1024]{2,1,0:T(8,128)(2,1)S(1)} async-done(((bf16[8,64,1024]{2,1,0:T(8,128)(2,1)}), bf16[8,64,1024]{2,1,0:T(8,128)(2,1)S(1)}, u32[]{:S(2)}, u32[]{:S(2)}) %all-to-all-start.1) | async-done | bytes 1048608 | tf_op jit(solution)/shard_map/all_to_all | solution.py:619
  28.7 0.0 copy-start.1
  28.7 3.6 all-to-all-start
  32.2 0.0 copy-done
  32.2 0.6 dynamic-slice_bitcast_fusion.bin_ref
  32.8 14.7 %all-to-all-done = bf16[8,64,1024]{2,1,0:T(8,128)(2,1)S(1)} async-done(((bf16[8,64,1024]{2,1,0:T(8,128)(2,1)}), bf16[8,64,1024]{2,1,0:T(8,128)(2,1)S(1)}, u32[]{:S(2)}, u32[]{:S(2)}) %all-to-all-start) | async-done | bytes 1048608 | tf_op jit(solution)/shard_map/all_to_all | solution.py:619
  47.6 0.0 copy-start.2
  47.6 0.0 copy-done.1
  47.6 1.0 copy-done.2
  48.5 390.7 %shard_map.178 = (bf16[512,1024]{1,0:T(8,128)(2,1)}, bf16[512,1024]{1,0:T(8,128)(2,1)}, f32[2,1024,1024]{2,1,0:T(8,128)}, f32[2,1024,1024]{2,1,0:T(8,128)}, f32[8,1024]{1,0:T(8,128)}, /*index=5*/f32[4,8,1024]{2,1,0:T(8,128)}) custom-call(bf16[512,1024]{1,0:T(8,128)(2,1)} %bitcast.44, bf16[512,1024]{1,0:T(8,128)(2,1)} %bitcast.43, f32[2,1024]{1,0:T(2,128)} %bitcast.54, ...), custom_call_target="tpu_custom_call" | custom-call | flops 68719476736 | bytes 20971520 | tf_op jit(solution)/shard_map/pallas_call | solution.py:541
  439.2 0.0 copy-start.3
  439.2 0.0 copy-start.4
  439.3 19.7 %all_to_all.46 = bf16[8,64,1024]{2,1,0:T(8,128)(2,1)S(1)} all-to-all(bf16[8,64,1024]{2,1,0:T(8,128)(2,1)} %bitcast.47), channel_id=1, replica_groups=mesh['rep'=4,'exp'=8] {'exp'}, dimensions={0} | all-to-all | bytes 2097152 | tf_op jit(solution)/shard_map/all_to_all | solution.py:622
  458.9 3.6 all-to-all-start.2
  462.5 0.0 copy-done.3
  462.5 0.6 slice.23
  463.1 1.5 slice.26
  464.6 0.6 slice_bitcast_fusion
  465.2 0.0 copy-done.4
  465.2 1.7 fusion.1
  467.0 10.9 %all-to-all-done.2 = bf16[8,64,1024]{2,1,0:T(8,128)(2,1)S(1)} async-done(((bf16[8,64,1024]{2,1,0:T(8,128)(2,1)}), bf16[8,64,1024]{2,1,0:T(8,128)(2,1)S(1)}, u32[]{:S(2)}, u32[]{:S(2)}) %all-to-all-start.2) | async-done | bytes 1048608 | tf_op jit(solution)/shard_map/all_to_all | solution.py:622
  477.8 0.0 slice-start
  477.8 3.1 add_convert_fusion
  480.9 0.0 slice-start.1
  480.9 8.6 %copy.22 = f32[1,2,1024,1024]{3,2,1,0:T(8,128)} copy(f32[1,2,1024,1024]{3,2,1,0:T(8,128)} %bitcast.42) | data formatting | bytes 16777216
  489.5 0.0 slice-done
  489.5 0.0 slice-done.1
  489.5 3.4 copy.23
  (5 shorter events, 0.1 us)
Async XLA Ops:
  0.6 31.6 %copy-start = (f32[1,2,4096]{2,1,0:T(2,128)S(1)}, f32[1,2,4096]{2,1,0:T(2,128)}, u32[]{:S(2)}) copy-start(f32[1,2,4096]{2,1,0:T(2,128)} %param.18) | copy-start | bytes 98308
  5.0 8.3 %copy-start.5 = (bf16[512,1024]{1,0:T(8,128)(2,1)S(1)}, bf16[512,1024]{1,0:T(8,128)(2,1)}, u32[]{:S(2)}) copy-start(bf16[512,1024]{1,0:T(8,128)(2,1)} %param.11) | copy-start | bytes 3145732
  8.1 20.6 %all-to-all-start.1 = ((bf16[8,64,1024]{2,1,0:T(8,128)(2,1)}), bf16[8,64,1024]{2,1,0:T(8,128)(2,1)S(1)}, u32[]{:S(2)}, u32[]{:S(2)}) async-start(bf16[8,64,1024]{2,1,0:T(8,128)(2,1)} %bitcast.6), calls=%async_computation.1 | async-start | bytes 2097152 | tf_op jit(solution)/shard_map/all_to_all | solution.py:619
  28.7 18.9 %copy-start.1 = (bf16[8,64,1024]{2,1,0:T(8,128)(2,1)}, bf16[8,64,1024]{2,1,0:T(8,128)(2,1)S(1)}, u32[]{:S(2)}) copy-start(bf16[8,64,1024]{2,1,0:T(8,128)(2,1)S(1)} %all-to-all-done.1) | copy-start | bytes 3145732
  28.7 18.9 %all-to-all-start = ((bf16[8,64,1024]{2,1,0:T(8,128)(2,1)}), bf16[8,64,1024]{2,1,0:T(8,128)(2,1)S(1)}, u32[]{:S(2)}, u32[]{:S(2)}) async-start(bf16[8,64,1024]{2,1,0:T(8,128)(2,1)} %bitcast.4), calls=%async_computation | async-start | bytes 2097152 | tf_op jit(solution)/shard_map/all_to_all | solution.py:619
  47.6 1.0 copy-start.2
  439.2 23.3 %copy-start.3 = (f32[8,1024]{1,0:T(8,128)S(1)}, f32[8,1024]{1,0:T(8,128)}, u32[]{:S(2)}) copy-start(f32[8,1024]{1,0:T(8,128)} %get-tuple-element.17) | copy-start | bytes 98308
  439.2 26.0 %copy-start.4 = (bf16[512,1024]{1,0:T(8,128)(2,1)S(1)}, bf16[512,1024]{1,0:T(8,128)(2,1)}, u32[]{:S(2)}) copy-start(bf16[512,1024]{1,0:T(8,128)(2,1)} %param.21) | copy-start | bytes 3145732
  458.9 18.9 %all-to-all-start.2 = ((bf16[8,64,1024]{2,1,0:T(8,128)(2,1)}), bf16[8,64,1024]{2,1,0:T(8,128)(2,1)S(1)}, u32[]{:S(2)}, u32[]{:S(2)}) async-start(bf16[8,64,1024]{2,1,0:T(8,128)(2,1)} %bitcast.14), calls=%async_computation.2 | async-start | bytes 2097152 | tf_op jit(solution)/shard_map/all_to_all | solution.py:622
  477.8 11.7 %slice-start = ((s8[8388608]{0:T(1024)(128)(4,1)}), s8[4194304]{0:T(1024)(128)(4,1)S(1)}, s32[]{:S(2)}) async-start(s8[8388608]{0:T(1024)(128)(4,1)} %bitcast.39), calls=%async_computation.4 | async-start | bytes 8388608
  480.9 8.6 %slice-start.1 = ((s8[8388608]{0:T(1024)(128)(4,1)}), s8[4194304]{0:T(1024)(128)(4,1)S(1)}, s32[]{:S(2)}) async-start(s8[8388608]{0:T(1024)(128)(4,1)} %bitcast.39), calls=%async_computation.5 | async-start | bytes 8388608

commit v3 on v2

--- a/solution.py
+++ b/solution.py
@@ -7,9 +7,6 @@
 from jax.experimental.pallas import tpu as pltpu
 from jax.sharding import PartitionSpec as P
 
-SLOT = 2048
-
-
 eps = 1e-05
 VMEM_BYTES = 60 * 1024 * 1024
 
@@ -52,56 +49,71 @@
     return jnp.sum(rows.reshape(rows.shape[0] // 8, 8, rows.shape[1]), 0)
 
 
-def kernel(
-    n,
-    x_ref,
-    dy_ref,
-    gain_ref,
-    nbias_ref,
-    cent_ref,
-    bin_ref,
-    bout_ref,
-    wi_hbm,
-    wo_hbm,
-    y_ref,
-    dv_ref,
-    gwi_hbm,
-    gwo_hbm,
-    sums_ref,
-    bins_ref,
-    gath,
-    wi,
-    wo,
-    gwi,
-    gwo,
-    part,
-    act,
-    dq,
-    slope,
-    total,
-    state,
-    dlog,
-    recv,
-    stage,
-    accs,
-    bacc,
-    mine,
-    peers,
-    send_sem,
-    recv_sem,
-    load_sem,
-    store_sem,
-    peer_send,
-    peer_recv,
-):
+def order_of(blocks):
+    if blocks == 1:
+        return [0]
+    others = [b for b in range(2, blocks, 2)] + [b for b in range(blocks - 1, 2, -2)]
+    return [0] + others + [1]
+
+
+def flip(index, bits):
+    out, place = index, 1
+    while place <= bits:
+        if bits & place:
+            out = out + place * (1 - 2 * lax.rem(index // place, 2))
+        place *= 2
+    return out
+
+
+def slot_rows(routes, blocks, cap):
+    rows = routes.shape[1]
+    along = routes.astype(jnp.float32)
+    table = lax.broadcasted_iota(jnp.int32, (max(blocks, 8), rows), 0).astype(jnp.float32)
+    hits = (table == along).astype(jnp.float32)
+    first = lax.broadcasted_iota(jnp.int32, (rows, rows), 0)
+    second = lax.broadcasted_iota(jnp.int32, (rows, rows), 1)
+    earlier = (first < second).astype(jnp.bfloat16)
+    before = jnp.dot(hits.astype(jnp.bfloat16), earlier, preferred_element_type=jnp.float32)
+    target = along * cap + jnp.sum(before * hits, 0, keepdims=True)
+    return (first.astype(jnp.float32) == target).astype(jnp.bfloat16)
+
+
+def live_rows(lengths_ref, device, devices, rows):
+    slot = rows * devices // lengths_ref.shape[0]
+    start = device * rows
+    count = lengths_ref[start // slot] - lax.rem(start, slot)
+    return (lax.broadcasted_iota(jnp.int32, (rows, 1), 0) < count).astype(jnp.float32)
+
+
+def kernel(n, blocks, inside, *refs):
+    refs = list(refs)
+    take = lambda count: [refs.pop(0) for _ in range(count)]
+    if inside:
+        tok_ref, cot_ref, routes_ref, lengths_ref = take(4)
+    else:
+        x_ref, dy_ref = take(2)
+    gain_ref, nbias_ref, cent_ref, bias_ref, bout_ref, wi_hbm, wo_hbm = take(7)
+    home_y, home_dv, gwi_hbm, gwo_hbm, cent_out, gain_out, nbias_out, bin_out, bout_out = take(9)
+    gath, wi, wo, gwi, gwo, part, act, dq, slope, total, state, dlog, recv, stage = take(14)
+    accs, bacc, mine, peers = take(4)
+    send_sem, recv_sem, load_sem, store_sem, peer_send, peer_recv = take(6)
+    if inside:
+        x_ref, dy_ref, y_ref, dv_ref, place, out_x, out_dy = take(7)
+        out_send, out_recv, home_send, home_recv, home_own = take(5)
+    else:
+        y_ref, dv_ref = home_y, home_dv
     r = lax.axis_index("rep")
+    e = lax.axis_index("exp")
     rows, width = x_ref.shape
-    hidden = bin_ref.shape[1]
+    hidden = wi_hbm.shape[2]
+    cap = rows // blocks
+    order = order_of(blocks)
+    per_chunk = blocks // CHUNKS
     chunk = rows // CHUNKS
     half = chunk // 2
     ops = 4 * CHUNKS
     rounds = ops + 1
-    block = min(32, chunk)
+    block = min(32, half)
     tile = min(512, hidden)
     wtile = hidden // 4
     last = n - 1
@@ -189,17 +201,84 @@
 
             copy(d, k, s, h, out, landing(d, k, s, h)).start()
 
-    def over_blocks(body):
+    def over_blocks(h, body):
         def step(b, carry):
-            body(pl.multiple_of(b * block, block))
+            body(pl.multiple_of(h * half + b * block, block))
             return carry
 
-        lax.fori_loop(0, chunk // block, step, 0)
+        lax.fori_loop(0, half // block, step, 0)
+
+    def cap_rows(q):
+        return pl.ds(pl.multiple_of(q * cap, cap), cap)
+
+    def outward(w, q):
+        src, dst = ((out_x, x_ref), (out_dy, dy_ref))[w]
+        return pltpu.make_async_remote_copy(
+            src_ref=src.at[cap_rows(q)],
+            dst_ref=dst.at[cap_rows(q)],
+            send_sem=out_send.at[w, q],
+            recv_sem=out_recv.at[w, q],
+            device_id={"exp": flip(e, order[q])},
+            device_id_type=MESH,
+        )
+
+    def homeward(w, q):
+        src, dst = ((y_ref, home_y), (dv_ref, home_dv))[w]
+        if q == 0:
+            return pltpu.make_async_copy(
+                src.at[cap_rows(q)], dst.at[cap_rows(e)], home_own.at[w]
+            )
+        return pltpu.make_async_remote_copy(
+            src_ref=src.at[cap_rows(q)],
+            dst_ref=dst.at[cap_rows(e)],
+            send_sem=home_send.at[w, q],
+            recv_sem=home_recv.at[w, q],
+            device_id={"exp": flip(e, order[q])},
+            device_id_type=MESH,
+        )
+
+    def dispatch(w):
+        for q in range(blocks):
+            expert = flip(e, order[q])
+            picked = place[cap_rows(expert), :]
+            source = tok_ref if w == 0 else cot_ref
+            values = source[...]
+            if w == 1:
+                device = r * blocks + e
+                values = (
+                    live_rows(lengths_ref, device, n * blocks, rows) * values.astype(jnp.float32)
+                ).astype(jnp.bfloat16)
+            ordered = jnp.dot(picked, values, preferred_element_type=jnp.float32)
+            target = ((x_ref, dy_ref) if q == 0 else (out_x, out_dy))[w]
+            target[cap_rows(q), :] = ordered.astype(jnp.bfloat16)
+            if q > 0:
+                if w == 0 and q == 1:
+                    pl.semaphore_wait(barrier, n - 1 + blocks - 1)
+                outward(w, q).start()
+
+    def each_block(c, h, body):
+        for chunk_at in range(CHUNKS):
+
+            @pl.when(c == chunk_at)
+            def _():
+                for q in range(
+                    chunk_at * per_chunk + h * (per_chunk // 2),
+                    chunk_at * per_chunk + (h + 1) * (per_chunk // 2),
+                ):
+                    body(q)
+
+    def arrived(w, c, h):
+        if inside:
+            each_block(c, h, lambda q: outward(w, q).wait_recv() if q > 0 else None)
+
+    def go_home(w, c, h):
+        if inside:
+            each_block(c, h, lambda q: homeward(w, q).start())
 
     def gate_of(x):
         return jax.nn.sigmoid(jnp.sum(x * cent_ref[...], -1, keepdims=True))
 
-    def prepare(i):
+    def prepare(i, h):
         kind, c, slot = op_type(i), op_chunk(i), op_slot(i)
 
         def own(offset, value):
@@ -210,7 +289,9 @@
 
         @pl.when(kind == 0)
         def _():
+            arrived(0, c, h)
             over_blocks(
+                h,
                 lambda o: own(
                     o,
                     layer_stats(x_ref[source(o), :].astype(jnp.float32))[0] * gain_ref[0:1, :]
@@ -221,6 +302,7 @@
         @pl.when(kind == 1)
         def _():
             over_blocks(
+                h,
                 lambda o: own(
                     o, layer_stats(state[source(o), :])[0] * gain_ref[1:2, :] + nbias_ref[1:2, :]
                 )
@@ -228,7 +310,9 @@
 
         @pl.when(kind == 2)
         def _():
+            arrived(1, c, h)
             over_blocks(
+                h,
                 lambda o: own(
                     o,
                     gate_of(x_ref[source(o), :].astype(jnp.float32))
@@ -238,7 +322,7 @@
 
         @pl.when(kind == 3)
         def _():
-            over_blocks(lambda o: own(o, state[source(o), :]))
+            over_blocks(h, lambda o: own(o, state[source(o), :]))
 
     def norm_back(values, grad, k):
         unit, scale = layer_stats(values)
@@ -251,7 +335,7 @@
             - unit * jnp.mean(through * unit, -1, keepdims=True)
         )
 
-    def finish(i):
+    def finish(i, h):
         kind, c = op_type(i), op_chunk(i)
 
         def source(offset):
@@ -266,7 +350,7 @@
                     + bout_ref[0:1, :]
                 )
 
-            over_blocks(body)
+            over_blocks(h, body)
 
         @pl.when(kind == 1)
         def _():
@@ -280,7 +364,8 @@
                 dlog[source(o), :] = jnp.broadcast_to(logit, (block, dlog.shape[1]))
                 accs[0] += fold(logit * x)
 
-            over_blocks(body)
+            over_blocks(h, body)
+            go_home(0, c, h)
 
         @pl.when(kind == 2)
         def _():
@@ -292,7 +377,7 @@
                 accs[5] += fold(middle)
                 accs[6] += fold(top)
 
-            over_blocks(body)
+            over_blocks(h, body)
 
         @pl.when(kind == 3)
         def _():
@@ -304,7 +389,8 @@
                     + dlog[source(o), 0:1] * cent_ref[...]
                 ).astype(jnp.bfloat16)
 
-            over_blocks(body)
+            over_blocks(h, body)
+            go_home(1, c, h)
 
     def over_tiles(count, size, body):
         def step(j, carry):
@@ -323,7 +409,7 @@
         def body(cs):
             inner = (
                 jnp.dot(gath[slot, p], wi[k, :, cs], preferred_element_type=jnp.float32)
-                + bin_ref[pl.ds(k, 1), cs]
+                + bias_ref[pl.ds(k, 1), pl.ds(pl.multiple_of(r * hidden + cs.start, tile), tile)]
             )
             low, pull = gelu_and_slope(inner)
             act[par, p, :, cs] = low.astype(jnp.bfloat16)
@@ -391,8 +477,16 @@
         )
     load(0).start()
     load(1).start()
-    prepare(0)
-    pl.semaphore_wait(barrier, n - 1)
+    if inside:
+        for b in range(1, blocks):
+            pl.semaphore_signal(
+                barrier, inc=1, device_id={"exp": flip(e, b)}, device_id_type=MESH
+            )
+        place[...] = slot_rows(routes_ref[...], blocks, cap)
+        dispatch(0)
+    else:
+        pl.semaphore_wait(barrier, n - 1)
+    prepare(0, 0)
 
     def step(t, carry):
         k, s = t // n, lax.rem(t, n)
@@ -430,6 +524,10 @@
 
         @pl.when(t == 0)
         def _():
+            prepare(0, 1)
+
+        @pl.when(t == 1)
+        def _():
             def clear(b, carry):
                 zero_rows = pl.ds(pl.multiple_of(b * 64, 64), 64)
                 for w in range(2):
@@ -441,6 +539,12 @@
             accs[...] = jnp.zeros_like(accs)
             bacc[...] = jnp.zeros_like(bacc)
 
+        if inside:
+
+            @pl.when(t == 2)
+            def _():
+                dispatch(1)
+
         @pl.when(t == n)
         def _():
             load(0).wait()
@@ -461,11 +565,13 @@
 
         @pl.when((s == 2) & (k >= 2))
         def _():
-            finish(k - 2)
+            for h in range(2):
+                finish(k - 2, h)
 
         @pl.when((s == 3) & (k < ops - 1))
         def _():
-            prepare(k + 1)
+            for h in range(2):
+                prepare(k + 1, h)
 
         @pl.when(t == n * (3 * CHUNKS + 1) + 2)
         def _():
@@ -488,7 +594,7 @@
         for d in range(2):
             wait_received(d, rounds - 1, n - 1, h)
         finish_sum(rounds - 1, h)
-    finish(ops - 1)
+        finish(ops - 1, h)
     for h in range(2):
         for d in range(2):
             for back in (2, 1):
@@ -513,23 +619,37 @@
 
     for q in range(1, n):
         tell(q).start()
+
+    def place_bins(q, bins):
+        bin_out[:, pl.ds(pl.multiple_of(q * hidden, hidden), hidden)] = bins
+
     sums = mine[0:8, :width]
-    bins_ref[r] = mine[8:16, :hidden]
+    place_bins(r, mine[8:10, :hidden])
     for q in range(1, n):
         tell(q).wait_recv()
         sums += peers[q - 1, 0:8, :width]
-        bins_ref[lax.rem(r - q + n, n)] = peers[q - 1, 8:16, :hidden]
-    sums_ref[...] = sums
+        place_bins(lax.rem(r - q + n, n), peers[q - 1, 8:10, :hidden])
+    cent_out[...] = sums[0:1]
+    gain_out[...] = sums[1:3]
+    nbias_out[...] = sums[3:5]
+    bout_out[...] = sums[5:7]
     for q in range(1, n):
         tell(q).wait_send()
+    if inside:
+        for w in range(2):
+            homeward(w, 0).wait()
+            for q in range(1, blocks):
+                outward(w, q).wait_send()
+                homeward(w, q).wait_send()
+                homeward(w, q).wait_recv()
     for w in range(2):
         for k in range(2):
             store(w, k).wait()
 
 
-def run_layer(x, dy, gains, nbias, cent, my_bias, bout, wi, wo):
-    n = lax.axis_size("rep")
-    rows, width = x.shape
+def run_layer(inside, rows_in, gains, nbias, cent, biases, bout, wi, wo):
+    n, blocks = lax.axis_size("rep"), lax.axis_size("exp")
+    rows, width = rows_in[0].shape
     hidden = wi.shape[2]
     chunk = rows // CHUNKS
     half = chunk // 2
@@ -537,19 +657,34 @@
     low, full = jnp.bfloat16, jnp.float32
     vmem = pl.BlockSpec(memory_space=pltpu.VMEM)
     anywhere = pl.BlockSpec(memory_space=pl.ANY)
+    home = anywhere if inside else vmem
+    row_specs = [vmem] * 2
+    extra = []
+    if inside:
+        row_specs = [vmem] * 3 + [pl.BlockSpec(memory_space=pltpu.SMEM)]
+        extra = (
+            [pltpu.VMEM((rows, width), low)] * 4
+            + [pltpu.VMEM((rows, rows), low)]
+            + [pltpu.VMEM((rows, width), low)] * 2
+            + [pltpu.SemaphoreType.DMA((2, blocks))] * 4
+            + [pltpu.SemaphoreType.DMA((2,))]
+        )
     flops = 2 * 16 * n * rows * width * hidden
     return pl.pallas_call(
-        functools.partial(kernel, n),
+        functools.partial(kernel, n, blocks, inside),
         out_shape=(
             jax.ShapeDtypeStruct((rows, width), low),
             jax.ShapeDtypeStruct((rows, width), low),
             jax.ShapeDtypeStruct((2, width, hidden), full),
             jax.ShapeDtypeStruct((2, hidden, width), full),
-            jax.ShapeDtypeStruct((8, width), full),
-            jax.ShapeDtypeStruct((n, 8, hidden), full),
+            jax.ShapeDtypeStruct((1, width), full),
+            jax.ShapeDtypeStruct((2, width), full),
+            jax.ShapeDtypeStruct((2, width), full),
+            jax.ShapeDtypeStruct((2, n * hidden), full),
+            jax.ShapeDtypeStruct((2, width), full),
         ),
-        in_specs=[vmem] * 7 + [anywhere] * 2,
-        out_specs=(vmem, vmem, anywhere, anywhere, vmem, vmem),
+        in_specs=row_specs + [vmem] * 5 + [anywhere] * 2,
+        out_specs=(home, home, anywhere, anywhere, vmem, vmem, vmem, vmem, vmem),
         scratch_shapes=[
             pltpu.VMEM((CHUNKS + POOL, n, chunk, width), low),
             pltpu.VMEM((2, width, hidden), low),
@@ -575,14 +710,89 @@
             pltpu.SemaphoreType.DMA((2, 2)),
             pltpu.SemaphoreType.DMA((n - 1,)),
             pltpu.SemaphoreType.DMA((n - 1,)),
-        ],
+        ]
+        + extra,
         compiler_params=pltpu.CompilerParams(
             collective_id=0, has_side_effects=True, vmem_limit_bytes=VMEM_BYTES
         ),
         cost_estimate=pl.CostEstimate(
             flops=flops, bytes_accessed=40 * rows * width, transcendentals=8 * rows * hidden * n
         ),
-    )(x, dy, gains, nbias, cent, my_bias, bout, wi, wo)
+    )(*rows_in, gains, nbias, cent, biases, bout, wi, wo)
+
+
+def close_kernel(device_count, cap, *refs):
+    tok_hbm, cot_hbm, routes_ref, lengths_ref, y_hbm, dv_hbm, gwi_in, gwo_in = refs[:8]
+    small_in, refs = refs[8:13], refs[13:]
+    mixed_ref, grad_ref, gwi_out, gwo_out = refs[:4]
+    small_out, refs = refs[4:9], refs[9:]
+    tok, cot, y, dv, hold_wi, hold_wo, load_sem, in_sem, out_sem = refs
+    rows = tok.shape[0]
+    pieces = in_sem.shape[1]
+    moves = []
+    for w, (src, hold, dst) in enumerate(
+        ((gwi_in, hold_wi, gwi_out), (gwo_in, hold_wo, gwo_out))
+    ):
+        depth = src.shape[1] * 2 // pieces
+        for j in range(pieces):
+            at = (j * 2 // pieces, pl.ds(j % (pieces // 2) * depth, depth))
+            moves.append(
+                (
+                    pltpu.make_async_copy(src.at[at], hold.at[at], in_sem.at[w, j]),
+                    pltpu.make_async_copy(hold.at[at], dst.at[at], out_sem.at[w, j]),
+                )
+            )
+    loads = [
+        pltpu.make_async_copy(src, dst, load_sem.at[j])
+        for j, (src, dst) in enumerate(((y_hbm, y), (dv_hbm, dv), (tok_hbm, tok), (cot_hbm, cot)))
+    ]
+    for copy in loads:
+        copy.start()
+    for fetch, _ in moves:
+        fetch.start()
+    for src, dst in zip(small_in, small_out):
+        dst[...] = src[...]
+    place = slot_rows(routes_ref[...], rows // cap, cap)
+    device = lax.axis_index("rep") * lax.axis_size("exp") + lax.axis_index("exp")
+    live = live_rows(lengths_ref, device, device_count, rows)
+    for copy in loads:
+        copy.wait()
+    for fetch, give in moves[:pieces]:
+        fetch.wait()
+        give.start()
+    mixed_ref[...] = (tok[...].astype(jnp.float32) + live * contract_rows(place, y[...])).astype(
+        jnp.bfloat16
+    )
+    for fetch, give in moves[pieces:]:
+        fetch.wait()
+        give.start()
+    grad_ref[...] = (cot[...].astype(jnp.float32) + contract_rows(place, dv[...])).astype(
+        jnp.bfloat16
+    )
+    for _, give in moves:
+        give.wait()
+
+
+def close(tokens, cotangent, routes, lengths, home_y, home_dv, gwi, gwo, *small):
+    n, blocks = lax.axis_size("rep"), lax.axis_size("exp")
+    rows, width = tokens.shape
+    vmem = pl.BlockSpec(memory_space=pltpu.VMEM)
+    anywhere = pl.BlockSpec(memory_space=pl.ANY)
+    rows_shape = jax.ShapeDtypeStruct(tokens.shape, tokens.dtype)
+    like = lambda a: jax.ShapeDtypeStruct(a.shape, a.dtype)
+    return pl.pallas_call(
+        functools.partial(close_kernel, n * blocks, rows // blocks),
+        out_shape=(rows_shape, rows_shape, like(gwi), like(gwo), *map(like, small)),
+        in_specs=[anywhere, anywhere, vmem, pl.BlockSpec(memory_space=pltpu.SMEM)]
+        + [anywhere] * 4
+        + [vmem] * 5,
+        out_specs=[vmem, vmem, anywhere, anywhere] + [vmem] * 5,
+        scratch_shapes=[pltpu.VMEM((rows, width), tokens.dtype)] * 4
+        + [pltpu.VMEM(gwi.shape, gwi.dtype), pltpu.VMEM(gwo.shape, gwo.dtype)]
+        + [pltpu.SemaphoreType.DMA((4,))]
+        + [pltpu.SemaphoreType.DMA((2, 8))] * 2,
+        compiler_params=pltpu.CompilerParams(vmem_limit_bytes=VMEM_BYTES),
+    )(tokens, cotangent, routes, lengths, home_y, home_dv, gwi, gwo, *small)
 
 
 def shards(
@@ -601,53 +811,59 @@
     n_exp = lax.axis_size("exp")
     tok_rows = tokens.shape[0]
     cap = tok_rows // n_exp
-    device = lax.axis_index(("rep", "exp"))
-    positions = device * tok_rows + lax.iota(jnp.int32, tok_rows)
-    seq_ids = positions // SLOT
-    seq_table = lax.iota(jnp.int32, lengths.shape[0])
-    seq_len = jnp.sum(jnp.where(seq_ids[:, None] == seq_table[None, :], lengths[None, :], 0), 1)
-    live = (positions % SLOT < seq_len).astype(jnp.float32)[:, None]
-    route = routes[:, 0]
-    hits = (route[:, None] == lax.iota(jnp.int32, n_exp)[None, :]).astype(jnp.int32)
-    before = jnp.cumsum(hits, 0) - hits
-    target = route * cap + jnp.sum(before * hits, 1)
-    place = (lax.iota(jnp.int32, tok_rows)[:, None] == target[None, :]).astype(jnp.bfloat16)
-    grad_out = (live * cotangent.astype(jnp.float32)).astype(jnp.bfloat16)
-
-    def send(rows):
-        ordered = jnp.dot(place, rows, preferred_element_type=jnp.float32).astype(jnp.bfloat16)
-        return lax.all_to_all(ordered, "exp", split_axis=0, concat_axis=0, tiled=True)
-
-    def give_back(rows):
-        back = lax.all_to_all(rows, "exp", split_axis=0, concat_axis=0, tiled=True)
-        return contract_rows(place, back)
-
-    ff = w_in.shape[3]
-    my_bias = lax.dynamic_slice_in_dim(in_biases[0], lax.axis_index("rep") * ff, ff, 1)
-    result, grad_local, w_in_grad, w_out_grad, sums, bins = run_layer(
-        send(tokens),
-        send(grad_out),
+    params = (
         norm_gains[0],
         norm_biases[0],
         centroids,
-        my_bias,
+        in_biases[0],
         out_biases[0],
         w_in[0],
         w_out[0],
     )
-    mixed = (tokens.astype(jnp.float32) + live * give_back(result)).astype(jnp.bfloat16)
-    tokens_grad = (cotangent.astype(jnp.float32) + give_back(grad_local)).astype(jnp.bfloat16)
-    in_bias_grad = jnp.transpose(bins[:, 0:2], (1, 0, 2)).reshape(1, 2, -1)
+    if cap % 16 == 0 and n_exp % (2 * CHUNKS) == 0:
+        row_routes = routes.reshape(1, tok_rows)
+        results = run_layer(True, (tokens, cotangent, row_routes, lengths), *params)
+        results = close(tokens, cotangent, row_routes, lengths, *results)
+    else:
+        device = lax.axis_index(("rep", "exp"))
+        slot = tok_rows * n_exp * lax.axis_size("rep") // lengths.shape[0]
+        positions = device * tok_rows + lax.iota(jnp.int32, tok_rows)
+        seq_ids = positions // slot
+        seq_table = lax.iota(jnp.int32, lengths.shape[0])
+        seq_len = jnp.sum(
+            jnp.where(seq_ids[:, None] == seq_table[None, :], lengths[None, :], 0), 1
+        )
+        live = (positions % slot < seq_len).astype(jnp.float32)[:, None]
+        route = routes[:, 0]
+        hits = (route[:, None] == lax.iota(jnp.int32, n_exp)[None, :]).astype(jnp.int32)
+        before = jnp.cumsum(hits, 0) - hits
+        target = route * cap + jnp.sum(before * hits, 1)
+        place = (lax.iota(jnp.int32, tok_rows)[:, None] == target[None, :]).astype(jnp.bfloat16)
+        grad_out = (live * cotangent.astype(jnp.float32)).astype(jnp.bfloat16)
+
+        def send(rows):
+            ordered = jnp.dot(place, rows, preferred_element_type=jnp.float32).astype(jnp.bfloat16)
+            return lax.all_to_all(ordered, "exp", split_axis=0, concat_axis=0, tiled=True)
+
+        def give_back(rows):
+            back = lax.all_to_all(rows, "exp", split_axis=0, concat_axis=0, tiled=True)
+            return contract_rows(place, back)
+
+        result, grad_local, *rest = run_layer(False, (send(tokens), send(grad_out)), *params)
+        mixed = (tokens.astype(jnp.float32) + live * give_back(result)).astype(jnp.bfloat16)
+        tokens_grad = (cotangent.astype(jnp.float32) + give_back(grad_local)).astype(jnp.bfloat16)
+        results = (mixed, tokens_grad, *rest)
+    mixed, tokens_grad, gwi, gwo, cent_grad, gain_grad, nbias_grad, bin_grad, bout_grad = results
     return (
         mixed,
         tokens_grad,
-        sums[0:1],
-        sums[1:3][None],
-        sums[3:5][None],
-        w_in_grad[None],
-        in_bias_grad,
-        w_out_grad[None],
-        sums[5:7][None],
+        cent_grad,
+        gain_grad[None],
+        nbias_grad[None],
+        gwi[None],
+        bin_grad[None],
+        gwo[None],
+        bout_grad[None],
     )
 
 

time: 493 us -> 414 us (0.84)
  waiting for transfers between devices: 39.3 us -> 0 us
  Pallas kernels: 391 us -> 413 us
  blocking collectives: 19.7 us -> 0 us
  local copies, waits for them, and re-layouts: 16.5 us -> 0 us
  starting transfers between devices: 12.3 us -> 0 us
  matrix products: 9.63 us -> 0 us
    all_to_all x3 -> x0, waiting for transfers between devices: 39.3 us -> none  [the longest x2 28.4 us: send(): lax.all_to_all(ordered, 'exp', split_axis=0, concat_axis=0, tiled=True)]
    pallas_call x1 -> x2, Pallas kernels: 391 us -> 413 us  [the longest x1 398 us: run_layer(): pl.pallas_call(functools.partial(kernel, n, blocks, inside), out_shape=(j...]
    all_to_all x1 -> x0, blocking collectives: 19.7 us -> none  [give_back(): back = lax.all_to_all(rows, 'exp', split_axis=0, concat_axis=0, tiled=True)]
    unnamed x18 -> x0, local copies, waits for them, and re-layouts: 13 us -> none
    all_to_all x3 -> x0, starting transfers between devices: 12.3 us -> none  [the longest x2 8.73 us: send(): lax.all_to_all(ordered, 'exp', split_axis=0, concat_axis=0, tiled=True)]
    dot_general x4 -> x0, matrix products: 9.63 us -> none  [the longest x2 4.84 us: contract_rows(): lax.dot_general(left, right, (((0,), (0,)), ((), ())), preferred_element_...]
  transfers between devices with their start and end apart: 3 -> 0, of which waited for: 3 -> 0; matrix products, arithmetic and copies ran while one was open for 1% -> 0% of each run, Pallas kernels for 0% -> 0%
where the time goes in v3:
time: 414 us
  Pallas kernels  413 us (100%)
    pallas_call x1, Pallas kernels, run_layer(): pl.pallas_call(functools.partial(kernel, n, blocks, inside), out_shape=(j...  398 us
    pallas_call x1, Pallas kernels, close(): pl.pallas_call(functools.partial(close_kernel, n * blocks, rows // blocks...  15 us

profile of v3, /device:TPU:0, one launch (start us, length us, event | category | flops | bytes accessed | tf_op | source)
XLA Modules:
  0.0 413.5 jit_solution(1837625909706366668)
XLA Ops:
  0.6 397.9 %shard_map.178 = (bf16[512,1024]{1,0:T(8,128)(2,1)}, bf16[512,1024]{1,0:T(8,128)(2,1)}, f32[2,1024,1024]{2,1,0:T(8,128)}, f32[2,1024,1024]{2,1,0:T(8,128)}, f32[...) custom-call(bf16[512,1024]{1,0:T(8,128)(2,1)} %refs_0_.3, ...), custom_call_target="tpu_custom_call" | custom-call | flops 68719476736 | bytes 20971520 | tf_op jit(solution)/shard_map/pallas_call | solution.py:673
  398.5 15.0 %shard_map.179 = (bf16[512,1024]{1,0:T(8,128)(2,1)}, bf16[512,1024]{1,0:T(8,128)(2,1)}, f32[2,1024,1024]{2,1,0:T(8,128)}, f32[2,1024,1024]{2,1,0:T(8,128)}, f32[...) custom-call(bf16[512,1024]{1,0:T(8,128)(2,1)} %refs_0_.3, ...), custom_call_target="tpu_custom_call" | custom-call | tf_op jit(solution)/shard_map/pallas_call | solution.py:783

commit v4 on v3

--- a/solution.py
+++ b/solution.py
@@ -8,7 +8,7 @@
 from jax.sharding import PartitionSpec as P
 
 eps = 1e-05
-VMEM_BYTES = 60 * 1024 * 1024
+VMEM_BYTES = 42 * 1024 * 1024
 
 
 def contract_rows(left, right):
@@ -89,17 +89,18 @@
     refs = list(refs)
     take = lambda count: [refs.pop(0) for _ in range(count)]
     if inside:
-        tok_ref, cot_ref, routes_ref, lengths_ref = take(4)
+        tok_ref, cot_hbm, routes_ref, lengths_ref = take(4)
     else:
         x_ref, dy_ref = take(2)
     gain_ref, nbias_ref, cent_ref, bias_ref, bout_ref, wi_hbm, wo_hbm = take(7)
-    home_y, home_dv, gwi_hbm, gwo_hbm, cent_out, gain_out, nbias_out, bin_out, bout_out = take(9)
-    gath, wi, wo, gwi, gwo, part, act, dq, slope, total, state, dlog, recv, stage = take(14)
-    accs, bacc, mine, peers = take(4)
-    send_sem, recv_sem, load_sem, store_sem, peer_send, peer_recv = take(6)
+    home_y, home_dv, gwi, gwo, cent_out, gain_out, nbias_out, bin_out, bout_out = take(9)
+    gath, wi, wo, part, act, dq, slope, total, state, dlog, recv, stage = take(12)
+    accs, bacc, mine, peers, mine_late, peers_late = take(6)
+    send_sem, recv_sem, load_sem, peer_send, peer_recv = take(5)
     if inside:
-        x_ref, dy_ref, y_ref, dv_ref, place, out_x, out_dy = take(7)
-        out_send, out_recv, home_send, home_recv, home_own = take(5)
+        x_ref, dy_ref, y_ref, dv_ref, place, cot_ref = take(6)
+        out_x, out_dy = y_ref, dv_ref
+        out_send, out_recv, home_send, home_recv, home_own, cot_sem = take(6)
     else:
         y_ref, dv_ref = home_y, home_dv
     r = lax.axis_index("rep")
@@ -237,17 +238,14 @@
             device_id_type=MESH,
         )
 
-    def dispatch(w):
-        for q in range(blocks):
-            expert = flip(e, order[q])
-            picked = place[cap_rows(expert), :]
-            source = tok_ref if w == 0 else cot_ref
-            values = source[...]
-            if w == 1:
-                device = r * blocks + e
-                values = (
-                    live_rows(lengths_ref, device, n * blocks, rows) * values.astype(jnp.float32)
-                ).astype(jnp.bfloat16)
+    def dispatch(w, first, stop):
+        values = (tok_ref, cot_ref)[w][...]
+        if w == 1:
+            device = r * blocks + e
+            live = live_rows(lengths_ref, device, n * blocks, rows)
+            values = (live * values.astype(jnp.float32)).astype(jnp.bfloat16)
+        for q in range(first, stop):
+            picked = place[cap_rows(flip(e, order[q])), :]
             ordered = jnp.dot(picked, values, preferred_element_type=jnp.float32)
             target = ((x_ref, dy_ref) if q == 0 else (out_x, out_dy))[w]
             target[cap_rows(q), :] = ordered.astype(jnp.bfloat16)
@@ -462,13 +460,46 @@
         base = jnp.where(near == 0, last - s, jnp.where(s < 2, last - s, s - 2))
         return jnp.where(r < 2, base, last - base)
 
+    def cot_load():
+        return pltpu.make_async_copy(cot_hbm, cot_ref, cot_sem)
+
+    EARLY, LATE = (0, 2, 4, 5, 6), (1, 3)
+
+    def tell(late, q):
+        src, dst = ((mine, peers), (mine_late, peers_late))[late]
+        return pltpu.make_async_remote_copy(
+            src_ref=src,
+            dst_ref=dst.at[q - 1],
+            send_sem=peer_send.at[late, q - 1],
+            recv_sem=peer_recv.at[late, q - 1],
+            device_id={"rep": lax.rem(r + q, n)},
+            device_id_type=MESH,
+        )
+
+    def tell_early():
+        for a, row in enumerate(EARLY):
+            mine[a : a + 1, :width] = jnp.sum(accs[row], 0, keepdims=True)
+        mine[5:6, :hidden] = jnp.sum(bacc[1], 0, keepdims=True)
+        mine[6:8, :] = jnp.zeros((2, mine.shape[1]), jnp.float32)
+        for q in range(1, n):
+            tell(0, q).start()
+
+    def tell_late():
+        at = 0
+        for values in (accs[LATE[0]], accs[LATE[1]], bacc[0]):
+            flat = jnp.sum(values, 0, keepdims=True)
+            for j in range(flat.shape[1] // 128):
+                mine_late[at : at + 1, :] = flat[:, j * 128 : (j + 1) * 128]
+                at += 1
+        for q in range(1, n):
+            tell(1, q).start()
+
+    def unpack(packed, at, size):
+        return jnp.concatenate([packed[at + j : at + j + 1] for j in range(size // 128)], 1)
+
     def load(w):
         src, dst = ((wi_hbm, wi), (wo_hbm, wo))[w]
         return pltpu.make_async_copy(src, dst, load_sem.at[w])
-
-    def store(w, k):
-        src, dst = ((gwi, gwi_hbm), (gwo, gwo_hbm))[w]
-        return pltpu.make_async_copy(src.at[k], dst.at[k], store_sem.at[w, k])
 
     barrier = pltpu.get_barrier_semaphore()
     for q in range(1, n):
@@ -482,8 +513,9 @@
             pl.semaphore_signal(
                 barrier, inc=1, device_id={"exp": flip(e, b)}, device_id_type=MESH
             )
+        cot_load().start()
         place[...] = slot_rows(routes_ref[...], blocks, cap)
-        dispatch(0)
+        dispatch(0, 0, 2)
     else:
         pl.semaphore_wait(barrier, n - 1)
     prepare(0, 0)
@@ -522,8 +554,14 @@
 
         exchange(0)
 
+        @pl.when(t == n * ops)
+        def _():
+            tell_early()
+
         @pl.when(t == 0)
         def _():
+            if inside:
+                dispatch(0, 2, blocks)
             prepare(0, 1)
 
         @pl.when(t == 1)
@@ -543,7 +581,14 @@
 
             @pl.when(t == 2)
             def _():
-                dispatch(1)
+                cot_load().wait()
+                dispatch(1, 0, blocks)
+
+            @pl.when(t == n * CHUNKS)
+            def _():
+                for w in range(2):
+                    for q in range(1, blocks):
+                        outward(w, q).wait_send()
 
         @pl.when(t == n)
         def _():
@@ -572,11 +617,6 @@
         def _():
             for h in range(2):
                 prepare(k + 1, h)
-
-        @pl.when(t == n * (3 * CHUNKS + 1) + 2)
-        def _():
-            store(0, 1).start()
-            store(1, 1).start()
 
         return carry
 
@@ -588,8 +628,6 @@
         return carry
 
     lax.fori_loop(0, 4, last_grads, 0)
-    store(0, 0).start()
-    store(1, 0).start()
     for h in range(2):
         for d in range(2):
             wait_received(d, rounds - 1, n - 1, h)
@@ -600,51 +638,42 @@
             for back in (2, 1):
                 wait_sent(d, (steps - back) // n, (steps - back) % n, h)
 
-    for a in range(7):
-        mine[a : a + 1, :width] = jnp.sum(accs[a], 0, keepdims=True)
-    mine[7:8, :] = jnp.zeros((1, mine.shape[1]), jnp.float32)
-    for k in range(2):
-        mine[8 + k : 9 + k, :hidden] = jnp.sum(bacc[k], 0, keepdims=True)
-    mine[10:16, :] = jnp.zeros((6, mine.shape[1]), jnp.float32)
-
-    def tell(q):
-        return pltpu.make_async_remote_copy(
-            src_ref=mine,
-            dst_ref=peers.at[q - 1],
-            send_sem=peer_send.at[q - 1],
-            recv_sem=peer_recv.at[q - 1],
-            device_id={"rep": lax.rem(r + q, n)},
-            device_id_type=MESH,
-        )
+    tell_late()
+
+    def place_bins(k, q, bins):
+        bin_out[k : k + 1, pl.ds(pl.multiple_of(q * hidden, hidden), hidden)] = bins
 
     for q in range(1, n):
-        tell(q).start()
-
-    def place_bins(q, bins):
-        bin_out[:, pl.ds(pl.multiple_of(q * hidden, hidden), hidden)] = bins
-
-    sums = mine[0:8, :width]
-    place_bins(r, mine[8:10, :hidden])
+        tell(0, q).wait_recv()
+    sums = mine[0:5, :width]
+    place_bins(1, r, mine[5:6, :hidden])
     for q in range(1, n):
-        tell(q).wait_recv()
-        sums += peers[q - 1, 0:8, :width]
-        place_bins(lax.rem(r - q + n, n), peers[q - 1, 8:10, :hidden])
+        sums += peers[q - 1, 0:5, :width]
+        place_bins(1, lax.rem(r - q + n, n), peers[q - 1, 5:6, :hidden])
     cent_out[...] = sums[0:1]
-    gain_out[...] = sums[1:3]
-    nbias_out[...] = sums[3:5]
-    bout_out[...] = sums[5:7]
+    gain_out[1:2, :] = sums[1:2]
+    nbias_out[1:2, :] = sums[2:3]
+    bout_out[...] = sums[3:5]
     for q in range(1, n):
-        tell(q).wait_send()
+        tell(1, q).wait_recv()
+    mine_rows = mine_late[...]
+    late = mine_rows[: 2 * width // 128]
+    place_bins(0, r, unpack(mine_rows, 2 * width // 128, hidden))
+    for q in range(1, n):
+        theirs = peers_late[q - 1]
+        late += theirs[: 2 * width // 128]
+        place_bins(0, lax.rem(r - q + n, n), unpack(theirs, 2 * width // 128, hidden))
+    gain_out[0:1, :] = unpack(late, 0, width)
+    nbias_out[0:1, :] = unpack(late, width // 128, width)
+    for q in range(1, n):
+        tell(0, q).wait_send()
+        tell(1, q).wait_send()
     if inside:
         for w in range(2):
             homeward(w, 0).wait()
             for q in range(1, blocks):
-                outward(w, q).wait_send()
                 homeward(w, q).wait_send()
                 homeward(w, q).wait_recv()
-    for w in range(2):
-        for k in range(2):
-            store(w, k).wait()
 
 
 def run_layer(inside, rows_in, gains, nbias, cent, biases, bout, wi, wo):
@@ -654,29 +683,29 @@
     chunk = rows // CHUNKS
     half = chunk // 2
     wide = max(width, hidden)
+    late = (2 * width + hidden) // 128
     low, full = jnp.bfloat16, jnp.float32
     vmem = pl.BlockSpec(memory_space=pltpu.VMEM)
     anywhere = pl.BlockSpec(memory_space=pl.ANY)
-    home = anywhere if inside else vmem
     row_specs = [vmem] * 2
     extra = []
     if inside:
-        row_specs = [vmem] * 3 + [pl.BlockSpec(memory_space=pltpu.SMEM)]
+        row_specs = [vmem, anywhere, vmem, pl.BlockSpec(memory_space=pltpu.SMEM)]
         extra = (
             [pltpu.VMEM((rows, width), low)] * 4
             + [pltpu.VMEM((rows, rows), low)]
-            + [pltpu.VMEM((rows, width), low)] * 2
+            + [pltpu.VMEM((rows, width), low)]
             + [pltpu.SemaphoreType.DMA((2, blocks))] * 4
-            + [pltpu.SemaphoreType.DMA((2,))]
+            + [pltpu.SemaphoreType.DMA((2,)), pltpu.SemaphoreType.DMA]
         )
     flops = 2 * 16 * n * rows * width * hidden
     return pl.pallas_call(
         functools.partial(kernel, n, blocks, inside),
         out_shape=(
-            jax.ShapeDtypeStruct((rows, width), low),
-            jax.ShapeDtypeStruct((rows, width), low),
-            jax.ShapeDtypeStruct((2, width, hidden), full),
-            jax.ShapeDtypeStruct((2, hidden, width), full),
+            pltpu.VMEM((rows, width), low) if inside else jax.ShapeDtypeStruct((rows, width), low),
+            pltpu.VMEM((rows, width), low) if inside else jax.ShapeDtypeStruct((rows, width), low),
+            pltpu.VMEM((2, width, hidden), full),
+            pltpu.VMEM((2, hidden, width), full),
             jax.ShapeDtypeStruct((1, width), full),
             jax.ShapeDtypeStruct((2, width), full),
             jax.ShapeDtypeStruct((2, width), full),
@@ -684,13 +713,11 @@
             jax.ShapeDtypeStruct((2, width), full),
         ),
         in_specs=row_specs + [vmem] * 5 + [anywhere] * 2,
-        out_specs=(home, home, anywhere, anywhere, vmem, vmem, vmem, vmem, vmem),
+        out_specs=(vmem, vmem, vmem, vmem, vmem, vmem, vmem, vmem, vmem),
         scratch_shapes=[
             pltpu.VMEM((CHUNKS + POOL, n, chunk, width), low),
             pltpu.VMEM((2, width, hidden), low),
             pltpu.VMEM((2, hidden, width), low),
-            pltpu.VMEM((2, width, hidden), full),
-            pltpu.VMEM((2, hidden, width), full),
             pltpu.VMEM((n, chunk, width), full),
             pltpu.VMEM((2, n, chunk, hidden), low),
             pltpu.VMEM((2, n, chunk, hidden), low),
@@ -702,14 +729,15 @@
             pltpu.VMEM((2, 2, 2, half, width), low),
             pltpu.VMEM((7, 8, width), full),
             pltpu.VMEM((2, 8, hidden), full),
-            pltpu.VMEM((16, wide), full),
-            pltpu.VMEM((n - 1, 16, wide), full),
+            pltpu.VMEM((8, wide), full),
+            pltpu.VMEM((n - 1, 8, wide), full),
+            pltpu.VMEM((late, 128), full),
+            pltpu.VMEM((n - 1, late, 128), full),
             pltpu.SemaphoreType.DMA((2, 2, 2)),
             pltpu.SemaphoreType.DMA((2, 2, n, 2)),
             pltpu.SemaphoreType.DMA((2,)),
-            pltpu.SemaphoreType.DMA((2, 2)),
-            pltpu.SemaphoreType.DMA((n - 1,)),
-            pltpu.SemaphoreType.DMA((n - 1,)),
+            pltpu.SemaphoreType.DMA((2, n - 1)),
+            pltpu.SemaphoreType.DMA((2, n - 1)),
         ]
         + extra,
         compiler_params=pltpu.CompilerParams(
@@ -722,34 +750,23 @@
 
 
 def close_kernel(device_count, cap, *refs):
-    tok_hbm, cot_hbm, routes_ref, lengths_ref, y_hbm, dv_hbm, gwi_in, gwo_in = refs[:8]
+    tok_hbm, cot_hbm, routes_ref, lengths_ref, y, dv, gwi_in, gwo_in = refs[:8]
     small_in, refs = refs[8:13], refs[13:]
     mixed_ref, grad_ref, gwi_out, gwo_out = refs[:4]
     small_out, refs = refs[4:9], refs[9:]
-    tok, cot, y, dv, hold_wi, hold_wo, load_sem, in_sem, out_sem = refs
+    tok, cot, load_sem, move_sem = refs
     rows = tok.shape[0]
-    pieces = in_sem.shape[1]
-    moves = []
-    for w, (src, hold, dst) in enumerate(
-        ((gwi_in, hold_wi, gwi_out), (gwo_in, hold_wo, gwo_out))
-    ):
-        depth = src.shape[1] * 2 // pieces
-        for j in range(pieces):
-            at = (j * 2 // pieces, pl.ds(j % (pieces // 2) * depth, depth))
-            moves.append(
-                (
-                    pltpu.make_async_copy(src.at[at], hold.at[at], in_sem.at[w, j]),
-                    pltpu.make_async_copy(hold.at[at], dst.at[at], out_sem.at[w, j]),
-                )
-            )
     loads = [
         pltpu.make_async_copy(src, dst, load_sem.at[j])
-        for j, (src, dst) in enumerate(((y_hbm, y), (dv_hbm, dv), (tok_hbm, tok), (cot_hbm, cot)))
+        for j, (src, dst) in enumerate(((tok_hbm, tok), (cot_hbm, cot)))
     ]
-    for copy in loads:
+    moves = [
+        pltpu.make_async_copy(src.at[k], dst.at[k], move_sem.at[w, k])
+        for w, (src, dst) in enumerate(((gwi_in, gwi_out), (gwo_in, gwo_out)))
+        for k in range(2)
+    ]
+    for copy in loads + moves:
         copy.start()
-    for fetch, _ in moves:
-        fetch.start()
     for src, dst in zip(small_in, small_out):
         dst[...] = src[...]
     place = slot_rows(routes_ref[...], rows // cap, cap)
@@ -757,20 +774,14 @@
     live = live_rows(lengths_ref, device, device_count, rows)
     for copy in loads:
         copy.wait()
-    for fetch, give in moves[:pieces]:
-        fetch.wait()
-        give.start()
     mixed_ref[...] = (tok[...].astype(jnp.float32) + live * contract_rows(place, y[...])).astype(
         jnp.bfloat16
     )
-    for fetch, give in moves[pieces:]:
-        fetch.wait()
-        give.start()
     grad_ref[...] = (cot[...].astype(jnp.float32) + contract_rows(place, dv[...])).astype(
         jnp.bfloat16
     )
-    for _, give in moves:
-        give.wait()
+    for copy in moves:
+        copy.wait()
 
 
 def close(tokens, cotangent, routes, lengths, home_y, home_dv, gwi, gwo, *small):
@@ -780,17 +791,17 @@
     anywhere = pl.BlockSpec(memory_space=pl.ANY)
     rows_shape = jax.ShapeDtypeStruct(tokens.shape, tokens.dtype)
     like = lambda a: jax.ShapeDtypeStruct(a.shape, a.dtype)
+    home_y, home_dv, gwi, gwo = (
+        pltpu.with_memory_space_constraint(a, pltpu.VMEM) for a in (home_y, home_dv, gwi, gwo)
+    )
     return pl.pallas_call(
         functools.partial(close_kernel, n * blocks, rows // blocks),
         out_shape=(rows_shape, rows_shape, like(gwi), like(gwo), *map(like, small)),
         in_specs=[anywhere, anywhere, vmem, pl.BlockSpec(memory_space=pltpu.SMEM)]
-        + [anywhere] * 4
-        + [vmem] * 5,
+        + [vmem] * 9,
         out_specs=[vmem, vmem, anywhere, anywhere] + [vmem] * 5,
-        scratch_shapes=[pltpu.VMEM((rows, width), tokens.dtype)] * 4
-        + [pltpu.VMEM(gwi.shape, gwi.dtype), pltpu.VMEM(gwo.shape, gwo.dtype)]
-        + [pltpu.SemaphoreType.DMA((4,))]
-        + [pltpu.SemaphoreType.DMA((2, 8))] * 2,
+        scratch_shapes=[pltpu.VMEM((rows, width), tokens.dtype)] * 2
+        + [pltpu.SemaphoreType.DMA((2,)), pltpu.SemaphoreType.DMA((2, 2))],
         compiler_params=pltpu.CompilerParams(vmem_limit_bytes=VMEM_BYTES),
     )(tokens, cotangent, routes, lengths, home_y, home_dv, gwi, gwo, *small)
 

time: 414 us -> 403 us (0.973)
  Pallas kernels: 413 us -> 402 us
    pallas_call x1, Pallas kernels: 15 us -> 8.16 us  [close(): pl.pallas_call(functools.partial(close_kernel, n * blocks, rows // blocks...]
where the time goes in v4:
time: 403 us
  Pallas kernels  402 us (100%)
    pallas_call x1, Pallas kernels, run_layer(): pl.pallas_call(functools.partial(kernel, n, blocks, inside), out_shape=(p...  394 us
    pallas_call x1, Pallas kernels, close(): pl.pallas_call(functools.partial(close_kernel, n * blocks, rows // blocks...  8.16 us

profile of v4, /device:TPU:0, one launch (start us, length us, event | category | flops | bytes accessed | tf_op | source)
XLA Modules:
  0.0 402.8 jit_solution(14957865099874728037)
XLA Ops:
  0.6 394.0 %shard_map.178 = (bf16[512,1024]{1,0:T(8,128)(2,1)S(1)}, bf16[512,1024]{1,0:T(8,128)(2,1)S(1)}, f32[2,1024,1024]{2,1,0:T(8,128)S(1)}, f32[2,1024,1024]{2,1,0:T(8...) custom-call(bf16[512,1024]{1,0:T(8,128)(2,1)} %refs_0_.3, ...), custom_call_target="tpu_custom_call" | custom-call | flops 68719476736 | bytes 20971520 | tf_op jit(solution)/shard_map/pallas_call | solution.py:702
  394.6 8.2 %shard_map.179 = (bf16[512,1024]{1,0:T(8,128)(2,1)}, bf16[512,1024]{1,0:T(8,128)(2,1)}, f32[2,1024,1024]{2,1,0:T(8,128)}, f32[2,1024,1024]{2,1,0:T(8,128)}, f32[...) custom-call(bf16[512,1024]{1,0:T(8,128)(2,1)} %refs_0_.3, ...), custom_call_target="tpu_custom_call" | custom-call | tf_op jit(solution)/shard_map/pallas_call | solution.py:797
